TPU v7x, 32 devices: a whole 2x2x4 slice. The times are simulated.
32 devices in a mesh: row: 4 (over y, x), col: 4 (over z), seq: 2 (over core).
Axes of the slice: x: 2, y: 2, z: 4, core: 2. Of those that a mesh axis runs over, the one named last changes fastest.
Arguments:
- alignment_tensor: bfloat16 [256, 128, 256], P('seq', ('row', 'col')), may hold values from -6 to 6
- occupancy_matrix: int32 [256, 128], P(None, ('row', 'col')), may hold values from 0 to 1, as said below
- first_factor_matrix: bfloat16 [256, 32], replicated, may hold values from -0.375 to 0.375
- second_factor_matrix: bfloat16 [256, 32], replicated, may hold values from -0.375 to 0.375
- couple_factor_matrix: bfloat16 [1024, 128], replicated, may hold values from -3 to 3
- couple_increment_adjoint: bfloat16 [128, 128, 128], P(('row', 'seq'), 'col'), may hold values from -6 to 6
Outputs:
- couple_increment: bfloat16 [128, 128, 128], P(('row', 'seq'), 'col')
- alignment_adjoint: bfloat16 [256, 128, 256], P('seq', ('row', 'col'))
- first_factor_adjoint: float32 [256, 32], replicated
- second_factor_adjoint: float32 [256, 32], replicated
- couple_factor_adjoint: float32 [1024, 128], replicated
Inputs may be any that keep to these rules, and one draw needn't show every extreme that they name: Row 0 of occupancy_matrix (the query) is all ones; every other sequence covers residues of one contiguous range with some gaps.
All inputs are finite; a program needn't handle non-finite values.
Results may differ from a plain program's by a relative error of at most 0.0076.
Values may be sent and summed in bfloat16 or wider, within the bound.
No kernel may reach another device: no remote copies, remote signals or barrier semaphores. Data moves between devices by JAX's collectives and lax.ppermute only.
A program may use at most 192 MiB of HBM per device.

v0:
```python
import jax
import jax.numpy as jnp
from jax import lax
from jax.sharding import PartitionSpec as P

ALIGN_DIM = 256
PROJ_DIM = 32
CZ = 128
OUTER = 1024


def broadcast(value, axis, root):
    mine = lax.axis_index(axis) == root
    return lax.psum(jnp.where(mine, value, jnp.zeros_like(value)), axis)


def local(
    alignment_tensor,
    occupancy_matrix,
    first_factor_matrix,
    second_factor_matrix,
    couple_factor_matrix,
    couple_increment_adjoint,
):
    homolog_shards = alignment_tensor.shape[0]
    embed_dimension = alignment_tensor.shape[1]
    seq_index = lax.axis_index("seq")
    col_index = lax.axis_index("col")
    argument_tensor = alignment_tensor.astype(jnp.float32)
    centered_input = argument_tensor - jnp.mean(argument_tensor, axis=-1, keepdims=True)
    reciprocal_spread = lax.rsqrt(
        jnp.mean(centered_input * centered_input, axis=-1, keepdims=True) + 1e-05
    )
    zscored_tensor = centered_input * reciprocal_spread
    rescaled_tensor = zscored_tensor.astype(jnp.bfloat16)
    raveled_matrix = rescaled_tensor.reshape(-1, ALIGN_DIM)
    maskf = occupancy_matrix.astype(jnp.float32)
    own_mask = lax.dynamic_slice_in_dim(maskf, seq_index * homolog_shards, homolog_shards, 0)
    left = (
        own_mask[:, :, None]
        * jnp.dot(raveled_matrix, first_factor_matrix, preferred_element_type=jnp.float32).reshape(
            homolog_shards, embed_dimension, PROJ_DIM
        )
    ).astype(jnp.bfloat16)
    right = (
        own_mask[:, :, None]
        * jnp.dot(raveled_matrix, second_factor_matrix, preferred_element_type=jnp.float32).reshape(
            homolog_shards, embed_dimension, PROJ_DIM
        )
    ).astype(jnp.bfloat16)
    stacked = jnp.concatenate([left, right], axis=2)
    both_rows, mask_rows = (
        lax.all_gather(stacked, "col", axis=1, tiled=True),
        lax.all_gather(occupancy_matrix.astype(jnp.bfloat16), "col", axis=1, tiled=True),
    )
    left_rows = both_rows[:, :, :PROJ_DIM]
    right_cols, mask_cols = (
        broadcast(both_rows[:, :, PROJ_DIM:], "row", lax.axis_index("col")),
        broadcast(mask_rows, "row", lax.axis_index("col")),
    )
    block = both_rows.shape[1]
    half = couple_increment_adjoint.shape[0]
    count = jnp.dot(mask_rows.T, mask_cols, preferred_element_type=jnp.float32)
    den = lax.dynamic_slice_in_dim(count, seq_index * half, half, 0) + 0.001
    wo32 = couple_factor_matrix.astype(jnp.float32)
    scaled = (couple_increment_adjoint.astype(jnp.float32) / den[:, :, None]).astype(jnp.bfloat16)
    lblock = left_rows
    outer = jnp.einsum("sic,sje->ijce", lblock, right_cols, preferred_element_type=jnp.float32)
    summed = lax.psum_scatter(
        outer.reshape(half * lax.axis_size("seq"), block, OUTER),
        "seq",
        scatter_dimension=0,
        tiled=True,
    )
    flat_outer = summed.reshape(-1, OUTER)
    projected = jnp.dot(flat_outer, wo32, precision=lax.Precision.HIGHEST).reshape(
        summed.shape[0], block, CZ
    )
    own_wo = jnp.dot(
        summed.reshape(-1, OUTER).T,
        scaled.astype(jnp.float32).reshape(-1, CZ),
        precision=lax.Precision.HIGHEST,
    )
    couple_increment = (projected / den[:, :, None]).astype(jnp.bfloat16)
    weight_t = couple_factor_matrix.T
    piece = lax.all_gather(scaled, "seq", axis=0, tiled=True)
    d_wo = own_wo
    number = piece.shape[0]
    d_outer = jnp.dot(piece.reshape(-1, CZ), weight_t, preferred_element_type=jnp.float32).astype(
        jnp.bfloat16
    )
    d_outer = d_outer.reshape(number, block, PROJ_DIM, PROJ_DIM)
    lblock = left_rows
    g_piece = jnp.einsum("ijce,sje->sic", d_outer, right_cols, preferred_element_type=jnp.float32)
    g_left = g_piece
    g_right = jnp.einsum("ijce,sic->sje", d_outer, lblock, preferred_element_type=jnp.float32)
    g_left_rows, g_right_cols, d_wo = (g_left, g_right, d_wo)
    left_total = lax.psum(g_left_rows, "col")
    g_left = lax.dynamic_slice_in_dim(left_total, col_index * embed_dimension, embed_dimension, 1)
    right_total = lax.psum(g_right_cols, "row")
    right_block = broadcast(right_total, "col", lax.axis_index("row"))
    g_right = lax.dynamic_slice_in_dim(right_block, col_index * embed_dimension, embed_dimension, 1)
    g_left = own_mask[:, :, None] * g_left
    g_right = own_mask[:, :, None] * g_right
    gl_flat = g_left.reshape(-1, PROJ_DIM)
    gr_flat = g_right.reshape(-1, PROJ_DIM)
    normed32 = raveled_matrix.astype(jnp.float32)
    first_factor_adjoint = jnp.dot(normed32.T, gl_flat, precision=lax.Precision.HIGHEST)
    second_factor_adjoint = jnp.dot(normed32.T, gr_flat, precision=lax.Precision.HIGHEST)
    rescaled_adjoint = jnp.dot(
        gl_flat, first_factor_matrix.astype(jnp.float32).T, precision=lax.Precision.HIGHEST
    )
    rescaled_adjoint = rescaled_adjoint + jnp.dot(
        gr_flat, second_factor_matrix.astype(jnp.float32).T, precision=lax.Precision.HIGHEST
    )
    rescaled_adjoint = rescaled_adjoint.reshape(homolog_shards, embed_dimension, ALIGN_DIM)
    addend_term = jnp.mean(rescaled_adjoint * zscored_tensor, axis=-1, keepdims=True)
    alignment_adjoint = (
        reciprocal_spread
        * (
            rescaled_adjoint
            - jnp.mean(rescaled_adjoint, axis=-1, keepdims=True)
            - zscored_tensor * addend_term
        )
    ).astype(jnp.bfloat16)
    subset_accumulations = lax.psum(
        (first_factor_adjoint, second_factor_adjoint, d_wo), ("row", "col", "seq")
    )
    return (
        couple_increment,
        alignment_adjoint,
        subset_accumulations[0],
        subset_accumulations[1],
        subset_accumulations[2],
    )


def solution(mesh):
    placed = (
        P("seq", ("row", "col"), None),
        P(None, ("row", "col")),
        P(),
        P(),
        P(),
        P(("row", "seq"), "col", None),
    )
    return jax.shard_map(
        local,
        mesh=mesh,
        in_specs=placed,
        out_specs=(P(("row", "seq"), "col", None), P("seq", ("row", "col"), None), P(), P(), P()),
        check_vma=False,
    )
```

profile of v0, /device:TPU:0, one launch (start us, length us, event | category | flops | bytes accessed | tf_op | source)
XLA Modules:
  0.0 593.6 jit_solution(13971093666773369096)
XLA Ops:
  7.2 0.7 dynamic-slice_convert_fusion
  8.0 0.1 copy.30
  8.1 1.3 convert_reduce_fusion
  9.4 1.4 fusion.12
  10.9 1.5 fusion.6
  12.4 0.5 fusion.5
  12.9 0.1 pad_maximum_fusion
  13.1 0.2 copy.31
  13.3 17.4 %all_gather.9 = bf16[128,32,64]{0,2,1:T(8,128)(2,1)S(1)} all-gather(bf16[128,8,64]{0,2,1:T(8,128)(2,1)S(1)} %copy.31), channel_id=1, replica_groups=mesh['row'=4,'col'=4,'seq'=2] {'col'}, dimensions={1}, use_global_device_ids=true | all-gather | bytes 655360 | tf_op jit(solution)/shard_map/all_gather | solution.py:53
  30.6 0.7 slice_select_fusion
  31.4 0.0 all-reduce.10.cloned.1.call-start
  31.5 13.4 %all_gather.10 = bf16[256,32]{0,1:T(8,128)(2,1)S(1)} all-gather(bf16[256,8]{0,1:T(8,128)(2,1)S(1)} %convert_element_type.43), channel_id=1, replica_groups=mesh['row'=4,'col'=4,'seq'=2] {'col'}, dimensions={1}, use_global_device_ids=true | all-gather | bytes 20480 | tf_op jit(solution)/shard_map/all_gather | solution.py:54
  44.9 16.1 %psum.57 = bf16[256,32]{0,1:T(8,128)(2,1)S(1)} all-reduce(bf16[256,32]{0,1:T(8,128)(2,1)S(1)} %broadcast_select_fusion.1), channel_id=1, replica_groups=mesh['row'=4,'col'=4,'seq'=2] {'row'}, use_global_device_ids=true, to_apply=%region_4.5 | all-reduce | flops 8192 | bytes 32768 | tf_op jit(solution)/shard_map/psum | solution.py:14
  61.0 0.1 fusion.37
  61.1 0.1 divide_convert_fusion
  61.3 2.0 all_gather.11
  63.3 0.7 convolution_convert_fusion
  64.0 7.9 %reshape.71 = bf16[32,32,32,32]{3,2,1,0:T(8,128)(2,1)} reshape(bf16[1024,1024]{1,0:T(8,128)(2,1)S(1)} %convolution_convert_fusion) | data formatting | bytes 4194304 | tf_op jit(solution)/shard_map/reshape | solution.py:92
  71.9 5.7 convolution_bitcast_fusion.1
  77.6 2.8 copy.35
  80.5 0.0 all-reduce.16.cloned.1.call-start
  80.6 5.9 convolution_bitcast_fusion.3
  86.4 2.8 copy.33
  89.2 60.6 %all-reduce.10.cloned.1.call-done = f32[128,32,32]{2,1,0:T(8,128)} async-done(((f32[128,32,32]{2,1,0:T(8,128)}), f32[128,32,32]{2,1,0:T(8,128)}) %all-reduce.10.cloned.1.call-update) | async-done | bytes 524304 | tf_op jit(solution)/shard_map/psum | solution.py:100
  149.9 3.2 broadcast_select_fusion
  153.1 0.2 reduce-scatter.2.cloned.1.call-start
  153.3 0.7 copy-done.3
  154.0 8.7 %convolution_bitcast_fusion = f32[32,32,32,32]{2,3,0,1:T(8,128)} fusion(bf16[128,32,32]{0,2,1:T(8,128)(2,1)S(1)} %copy-done.3, bf16[128,32,64]{0,2,1:T(8,128)(2,1)S(1)} %all_gather.9), kind=kOutput, calls=%fused_computation | convolution fusion | flops 268435456 | bytes 4718592 | tf_op jit(solution)/shard_map/sic,sje->ijce/dot_general | solution.py:68
  162.7 17.5 %copy.32 = f32[32,32,32,32]{3,2,1,0:T(8,128)} copy(f32[32,32,32,32]{2,3,0,1:T(8,128)} %convolution_bitcast_fusion) | data formatting | bytes 8388608 | tf_op jit(solution)/shard_map/sic,sje->ijce/transpose | solution.py:68
  180.2 13.7 %reshape.69 = f32[32,32,1024]{2,1,0:T(8,128)} reshape(f32[32,32,32,32]{3,2,1,0:T(8,128)} %copy.32) | data formatting | bytes 8388608 | tf_op jit(solution)/shard_map/reshape | solution.py:70
  193.9 0.0 all-reduce.14.cloned.1.call-start
  194.0 114.6 %all-reduce.16.cloned.1.call-done = (f32[128,32,32]{2,1,0:T(8,128)}, f32[128,32,32]{2,1,0:T(8,128)}) async-done(((f32[128,32,32]{2,1,0:T(8,128)}, f32[128,32,32]{2,1,0:T(8,128)}), (f32[128,32,32]{2,1,0:T(8,128)}, f32[128,32,32]{2,1,0:T(8,128)})) %all-reduce.16.cloned.1.call-update) | async-done | bytes 1048592 | tf_op jit(solution)/shard_map/psum | solution.py:98
  308.6 1.7 fusion.14
  310.3 1.8 fusion.8
  312.1 0.2 reduce_sum.38
  312.3 0.1 div.34
  312.4 2.7 convolution_bitcast_fusion.5
  315.1 2.9 convolution_bitcast_fusion.4
  318.0 1.4 fusion.11
  319.5 0.0 all-reduce.12.cloned.1.call-start
  319.5 2.4 reduce-scatter.2.cloned.1.call-done
  321.9 4.3 convolution_bitcast_fusion.2
  326.3 1.7 fusion.7
  328.0 119.4 %all-reduce.14.cloned.1.call-done = (f32[256,32]{0,1:T(8,128)}, f32[256,32]{0,1:T(8,128)}) async-done(((f32[256,32]{0,1:T(8,128)}, f32[256,32]{0,1:T(8,128)}), (f32[256,32]{0,1:T(8,128)}, f32[256,32]{0,1:T(8,128)})) %all-reduce.14.cloned.1.call-update) | async-done | bytes 65552 | tf_op jit(solution)/shard_map/psum | solution.py:126
  447.4 134.8 %all-reduce.12.cloned.1.call-done = f32[1024,128]{1,0:T(8,128)} async-done(((f32[1024,128]{1,0:T(8,128)}), f32[1024,128]{1,0:T(8,128)}) %all-reduce.12.cloned.1.call-update) | async-done | bytes 524304 | tf_op jit(solution)/shard_map/psum | solution.py:126
  582.2 1.4 copy.48
  583.5 1.4 copy.49
  584.9 1.9 copy.50
  (40 shorter events, 0.3 us)
Async XLA Ops:
  7.2 56.1 %copy-start = (bf16[1024,128]{1,0:T(8,128)(2,1)S(1)}, bf16[1024,128]{1,0:T(8,128)(2,1)}, u32[]{:S(2)}) copy-start(bf16[1024,128]{1,0:T(8,128)(2,1)} %param.10) | copy-start | bytes 786436
  7.2 73.4 %all-reduce.8.cloned.1.call-start = ((), (), s32[]{:S(2)}) async-start(), calls=%async_computation.1 | async-start | bytes 524288 | tf_op jit(solution)/shard_map/psum | solution.py:14
  8.1 4.3 copy-start.4
  8.1 4.3 copy-start.1
  8.1 4.3 copy-start.10
  12.4 19.0 %copy-start.9 = (s32[256,8]{0,1:T(8,128)S(1)}, s32[256,8]{0,1:T(8,128)}, u32[]{:S(2)}) copy-start(s32[256,8]{0,1:T(8,128)} %param.7) | copy-start | bytes 24580
  12.9 48.2 %copy-start.8 = (bf16[16,32,128]{2,1,0:T(8,128)(2,1)S(1)}, bf16[16,32,128]{2,1,0:T(8,128)(2,1)}, u32[]{:S(2)}) copy-start(bf16[16,32,128]{2,1,0:T(8,128)(2,1)} %param.11) | copy-start | bytes 393220
  31.4 118.5 %all-reduce.10.cloned.1.call-start = ((), (), s32[]{:S(2)}) async-start(), calls=%async_computation.3 | async-start | bytes 4194304 | tf_op jit(solution)/shard_map/psum | solution.py:100
  61.2 2.0 copy-start.6
  80.5 228.1 %all-reduce.16.cloned.1.call-start = ((), (), s32[]{:S(2)}) async-start(), calls=%async_computation.6 | async-start | bytes 8388608 | tf_op jit(solution)/shard_map/psum | solution.py:98
  153.1 0.9 copy-start.3
  153.1 168.8 %reduce-scatter.2.cloned.1.call-start = ((), (), s32[]{:S(2)}) async-start(), calls=%async_computation.2 | async-start | bytes 6291456 | tf_op jit(solution)/shard_map/reduce_scatter | solution.py:69
  193.9 114.7 %copy-start.5 = (f32[128,8]{1,0:T(8,128)S(1)}, f32[128,8]{1,0:T(8,128)}, u32[]{:S(2)}) copy-start(f32[128,8]{1,0:T(8,128)} %copy-done.4) | copy-start | bytes 12292
  193.9 114.7 %copy-start.11 = (bf16[256,32]{0,1:T(8,128)(2,1)S(1)}, bf16[256,32]{0,1:T(8,128)(2,1)}, u32[]{:S(2)}) copy-start(bf16[256,32]{0,1:T(8,128)(2,1)} %param.8) | copy-start | bytes 49156
  193.9 116.3 %copy-start.12 = (bf16[256,32]{0,1:T(8,128)(2,1)S(1)}, bf16[256,32]{0,1:T(8,128)(2,1)}, u32[]{:S(2)}) copy-start(bf16[256,32]{0,1:T(8,128)(2,1)} %param.9) | copy-start | bytes 49156
  193.9 253.5 %all-reduce.14.cloned.1.call-start = ((), (), s32[]{:S(2)}) async-start(), calls=%async_computation.5 | async-start | bytes 131072 | tf_op jit(solution)/shard_map/psum | solution.py:126
  315.1 6.8 %copy-start.7 = (bf16[16,32,128]{2,1,0:T(8,128)(2,1)S(1)}, bf16[16,32,128]{2,1,0:T(8,128)(2,1)}, u32[]{:S(2)}) copy-start(bf16[16,32,128]{2,1,0:T(8,128)(2,1)} %copy-done.6) | copy-start | bytes 393220
  319.5 262.7 %all-reduce.12.cloned.1.call-start = ((), (), s32[]{:S(2)}) async-start(), calls=%async_computation.4 | async-start | bytes 1048576 | tf_op jit(solution)/shard_map/psum | solution.py:126
  321.9 4.4 copy-start.2
Sparse Core Ops, SparseCore 0:
  31.5 44.6 all-reduce.7
  80.6 69.2 all-reduce.9
  153.2 155.3 all-reduce.15
  310.8 11.0 reduce-scatter.1
  328.0 119.3 all-reduce.13
  453.1 129.0 all-reduce.11
where the time goes:
time: 595 us; the launch traced here: 594 us
  waiting for transfers between devices  432 us (73%)
  local copies, waits for them, and re-layouts  50.5 us (8%)
  blocking collectives  48.9 us (8%)
  matrix products  38.3 us (6%)
  between operations  14.4 us (2%)
  other arithmetic  9.3 us (2%)
    psum x2, waiting for transfers between devices, local(): lax.psum((first_factor_adjoint, second_factor_adjoint, d_wo), ('row', 'co...  254 us
    psum x1, waiting for transfers between devices, local(): left_total = lax.psum(g_left_rows, 'col')  115 us
    psum x1, waiting for transfers between devices, local(): right_total = lax.psum(g_right_cols, 'row')  60.6 us
    transpose x1, local copies, waits for them, and re-layouts, local(): jnp.einsum('sic,sje->ijce', lblock, right_cols, preferred_element_type=jn...  17.5 us
    all_gather x1, blocking collectives, local(): lax.all_gather(stacked, 'col', axis=1, tiled=True)  17.4 us
    psum x1, blocking collectives, broadcast(): return lax.psum(jnp.where(mine, value, jnp.zeros_like(value)), axis)  16.1 us
    reshape x1, local copies, waits for them, and re-layouts, local(): outer.reshape(half * lax.axis_size('seq'), block, OUTER)  13.7 us
    all_gather x1, blocking collectives, local(): lax.all_gather(occupancy_matrix.astype(jnp.bfloat16), 'col', axis=1, tile...  13.4 us
  transfers between devices with their start and end apart: 6, of which 5 were waited for; matrix products, arithmetic and copies ran while one was open for 14% of the time, Pallas kernels for 0%

commit v1 on v0

v1 whole, which is shorter than its diff:
```python
import functools
import math

import jax
import jax.numpy as jnp
from jax import lax
from jax.experimental import pallas as pl
from jax.experimental.pallas import tpu as pltpu
from jax.sharding import PartitionSpec as P

ALIGN = 256
PROJ = 32
CZ = 128
OUTER = 1024
PAD = 16
AXES = ("row", "col", "seq")
BF = jnp.bfloat16
F32 = jnp.float32

NN = (((1,), (0,)), ((), ()))
NT = (((1,), (1,)), ((), ()))
TN = (((0,), (0,)), ((), ()))


def dot(a, b, dims):
    return lax.dot_general(a, b, dims, preferred_element_type=F32)


def normalize(x):
    centered = x - jnp.mean(x, axis=-1, keepdims=True)
    rstd = lax.rsqrt(jnp.mean(centered * centered, axis=-1, keepdims=True) + 1e-05)
    return centered * rstd, rstd


def strided(ref, place):
    return jnp.concatenate([ref[0, place, :], ref[1, place, :]], axis=1)


def own_mask(mask_ref, seqs):
    start = pl.multiple_of(lax.axis_index("seq") * seqs, seqs)
    return mask_ref[:, pl.ds(start, seqs)].astype(F32)


def norm_kernel(x_ref, normed_ref, token_ref, rows):
    q, seqs, _ = normed_ref.shape
    xhat = normalize(x_ref[...].astype(F32))[0]
    rows[0], rows[1] = xhat[:, :128], xhat[:, 128:]
    for i in range(q):
        normed_ref[i] = strided(rows, pl.ds(i, seqs, stride=q)).astype(BF)
    token_ref[...] = jnp.zeros_like(token_ref)


def copy_all(pairs, sems):
    copies = [pltpu.make_async_copy(a, b, sems.at[k]) for k, (a, b) in enumerate(pairs)]
    for copy in copies:
        copy.start()
    return copies


def project_kernel(
    x_hbm, mask_hbm, wl_hbm, wr_hbm, adj_hbm,
    right_hbm, *refs
):
    *col_hbm, x_ref, mask_ref, wl_ref, wr_ref, adj_ref, right_ref, left_ref, pairs_ref, rows, spread, sems = refs
    q, seqs = mask_ref.shape[0], right_ref.shape[1]
    n_col = len(col_hbm)
    col = lax.axis_index("col")
    chunk = q * PROJ
    held = ((adj_hbm, adj_ref), (x_hbm, x_ref), (mask_hbm, mask_ref), (wl_hbm, wl_ref), (wr_hbm, wr_ref))
    loads = copy_all(held, sems)
    loads[0].wait()
    pairs = adj_ref[...].astype(F32).reshape(-1, n_col, q, CZ)
    for p in range(n_col):
        pairs_ref[p] = pairs[:, p].reshape(-1, CZ).astype(BF)
    place, rest = pl.ds(0, chunk + PAD), pl.ds(chunk + PAD, pairs_ref.shape[1])
    sent = copy_all(
        [(pairs_ref.at[col ^ k], hbm.at[rest, :]) for k, hbm in enumerate(col_hbm)],
        sems.at[pl.ds(6 + n_col, n_col)],
    )
    for copy in loads[1:]:
        copy.wait()
    xhat = normalize(x_ref[...].astype(F32))[0]
    rows[0], rows[1] = xhat[:, :128], xhat[:, 128:]
    mask = own_mask(mask_ref, seqs)
    weights = jnp.concatenate([wl_ref[...], wr_ref[...]], axis=0)
    for i in range(q):
        mine = strided(rows, pl.ds(i, seqs, stride=q)).astype(BF)
        both = dot(weights, mine, NT) * mask[i : i + 1, :]
        left_ref[i * PROJ : (i + 1) * PROJ, :] = both[:PROJ].astype(BF)
        spread[pl.ds(i, PROJ, stride=q), :] = both[PROJ:]
    whole = mask_ref[...].astype(F32)
    halves = [whole[:, t * seqs : (t + 1) * seqs] for t in range(whole.shape[1] // seqs)]
    tail = jnp.concatenate(halves, axis=0).astype(BF)
    left_ref[chunk:, :] = tail
    right_ref[...] = jnp.concatenate([spread[...].astype(BF), tail], axis=0)
    sent += copy_all(
        [(right_ref, right_hbm)]
        + [(left_ref, hbm.at[place, :]) for hbm in col_hbm],
        sems.at[pl.ds(5, n_col + 1)],
    )
    for copy in sent:
        copy.wait()


def far_first(count):
    return sorted(range(count), key=lambda k: (k & 2) == 0)


def by_partner(refs):
    return [refs[far_first(len(refs)).index(k)] for k in range(len(refs))]


def sent_order(values):
    return [values[k] for k in far_first(len(values))]


def unpack_mask(tail, q):
    tail = tail.astype(F32)
    return jnp.concatenate([tail[t * q : (t + 1) * q] for t in range(tail.shape[0] // q)], axis=1)


def pack_kernel(n_row, ready_ref, *refs):
    *ins, mine_ref, theirs_ref, mask_right, mask_left, adj_ref, left_ref, masks_ref = refs
    cols, rights = ins[:-n_row][::-1], ins[-n_row:]
    half, chunk = len(cols) // 2, mine_ref.shape[1]
    size, q = chunk + PAD, mask_right.shape[0] // n_row
    row, col, seq = (lax.axis_index(name) for name in AXES)
    for k, ref in enumerate(rights):
        mine_ref[row ^ k] = ref[:chunk, :]
        theirs_ref[row ^ k] = ref[:chunk, :]
        mask_right[pl.ds(pl.multiple_of((row ^ k) * q, q), q), :] = unpack_mask(ref[chunk:, :], q)
    for k, ref in enumerate(cols):
        left_ref[col ^ k] = ref[:chunk, :]
        masks_ref[col ^ k] = unpack_mask(ref[chunk:size, :], q)
        adj_ref[col ^ k] = ref[size:, :]
    for k in range(half):
        mine_ref[n_row + k] = left_ref[seq * half + k]
        theirs_ref[n_row + k] = left_ref[(1 - seq) * half + k]
        mask_left[k * q : (k + 1) * q, :] = masks_ref[seq * half + k]


def exchange(blocks):
    lane = lax.broadcasted_iota(jnp.int32, blocks[0].shape, 1)
    even = (lane & 32) == 0
    low = lane < 64
    a = list(blocks)
    for p in (0, 2):
        first, second = a[p], a[p + 1]
        a[p] = jnp.where(even, first, pltpu.roll(second, 32, 1))
        a[p + 1] = jnp.where(even, pltpu.roll(first, 96, 1), second)
    for p in (0, 1):
        first, second = a[p], a[p + 2]
        a[p] = jnp.where(low, first, pltpu.roll(second, 64, 1))
        a[p + 2] = jnp.where(low, pltpu.roll(first, 64, 1), second)
    return a


def back_kernel(
    wp, mr, ml, adj_ref, mine, dd, scaled_ref, recip_ref, rt_ref, d3
):
    n_col, pairs, _ = adj_ref.shape
    rows_i, depth = ml.shape
    rows_j, q = mr.shape[0], pairs // rows_i
    mask_r = mr[...]
    both = jnp.concatenate([(ml[i : i + 1, :] * mask_r).astype(BF) for i in range(rows_i)], axis=0)
    count = dot(both, jnp.ones((depth, CZ), BF), NN)
    recip = 1.0 / (count + 0.001)
    recip_ref[...] = recip
    adjoint = jnp.stack(
        [adj_ref[p].astype(F32).reshape(rows_i, q, CZ) for p in range(n_col)], axis=1
    ).reshape(rows_i * rows_j, CZ)
    scaled = (adjoint * recip).astype(BF)
    scaled_ref[...] = scaled.astype(F32).T.astype(BF)
    rt_ref[...] = by_channel(mine, mr.shape[0] // q, q)
    d3[...] = dot(scaled, wp[...], NT)
    for g in range(PROJ // 4):
        for ig in range(rows_i // 4):
            blocks = [
                d3[(ig * 4 + b) * rows_j : (ig * 4 + b + 1) * rows_j, g * 128 : (g + 1) * 128]
                for b in range(4)
            ]
            for e, value in enumerate(exchange(blocks)):
                row = (g * 4 + e) * rows_j
                dd[row : row + rows_j, ig * 128 : (ig + 1) * 128] = value.astype(BF)


def by_channel(packed, n_row, q):
    blocks = [packed[r].astype(F32).reshape(PROJ, q, -1) for r in range(n_row)]
    return jnp.concatenate(blocks, axis=1).reshape(PROJ * n_row * q, -1).astype(BF)


def left_kernel(rt_mine, theirs, dd, rt, mine_ref, theirs_ref, parts):
    half, chunk, seqs = mine_ref.shape
    n_row, q = theirs.shape[0] - half, chunk // PROJ
    seq = lax.axis_index("seq")
    rt[:, pl.ds(pl.multiple_of(seq * seqs, seqs), seqs)] = rt_mine[...]
    rt[:, pl.ds(pl.multiple_of((1 - seq) * seqs, seqs), seqs)] = by_channel(theirs, n_row, q)
    g_left = dot(dd[...], rt[...], TN)
    for t in range(2):
        for k in range(half):
            part = g_left[k * chunk : (k + 1) * chunk, t * seqs : (t + 1) * seqs]
            parts[t, k] = part.astype(BF)
    mine_ref[...] = parts[seq]
    theirs_ref[...] = parts[1 - seq]


def pair_kernel(
    rt, wp, dd, scaled_ref, recip_ref, mine, theirs,
    mine_ref, theirs_ref, couple_ref,
    lt, wf, o3, parts,
):
    n_col, pairs, _ = couple_ref.shape
    _, chunk, seqs = mine.shape
    q = chunk // PROJ
    half = n_col // 2
    rows_i = half * q
    rows_j = dd.shape[0] // PROJ
    n_row = rows_j // q
    depth = rt.shape[1]
    seq = lax.axis_index("seq")
    for ref, side in ((mine, seq), (theirs, 1 - seq)):
        lanes = pl.ds(pl.multiple_of(side * seqs, seqs), seqs)
        for k in range(half):
            lt[k * chunk : (k + 1) * chunk, lanes] = ref[n_row + k]
    for g in range(PROJ // 4):
        part = dot(rt[g * 4 * rows_j : (g + 1) * 4 * rows_j, :], lt[...], NT)
        for ig in range(rows_i // 4):
            lanes = slice(ig * 128, (ig + 1) * 128)
            blocks = [part[e * rows_j : (e + 1) * rows_j, lanes] for e in range(4)]
            for b, value in enumerate(exchange(blocks)):
                i = ig * 4 + b
                o3[i * rows_j : (i + 1) * rows_j, g * 128 : (g + 1) * 128] = value.astype(BF)
    couple = (dot(o3[...], wp[...], NN) * recip_ref[...]).reshape(rows_i, n_col, q, CZ)
    for p in range(n_col):
        couple_ref[p] = couple[:, p].reshape(pairs, CZ).astype(BF)
    dwo = dot(scaled_ref[...], o3[...], NN).T
    for e in range(PROJ):
        wf[pl.ds(e, PROJ, stride=PROJ), :] = dwo[e * PROJ : (e + 1) * PROJ, :]
    split = OUTER // 2 // chunk
    g_right = dot(dd[...], lt[...], NN).reshape(PROJ, rows_j, depth)
    for t in range(2):
        lanes = slice(t * seqs, (t + 1) * seqs)
        for r in range(n_row):
            parts[t, r] = g_right[:, r * q : (r + 1) * q, lanes].reshape(chunk, seqs).astype(BF)
        for k in range(split):
            row = (t * split + k) * chunk
            parts[t, n_row + k] = wf[row : row + chunk, :].astype(BF)
    mine_ref[...] = parts[seq]
    theirs_ref[...] = parts[1 - seq]


def merge_left_kernel(mine_ref, got_ref, couple_ref, held_ref, passed_ref, *refs):
    *outs, left_ref = refs
    passed_ref[...] = held_ref[...]
    half, chunk, _ = mine_ref.shape
    col, seq = lax.axis_index("col"), lax.axis_index("seq")
    for k in range(half):
        left_ref[seq * half + k] = mine_ref[k]
        left_ref[(1 - seq) * half + k] = got_ref[k]
    for k, ref in enumerate(outs):
        ref[:chunk, :] = left_ref[col ^ k]
        ref[chunk:, :] = couple_ref[col ^ k]


def merge_right_kernel(mine_ref, got_ref, *refs):
    *outs, dwo_ref = refs
    n_row, chunk = len(outs), mine_ref.shape[1]
    row = lax.axis_index("row")
    dwo = mine_ref[n_row:].astype(F32) + got_ref[n_row:].astype(F32)
    dwo_ref[...] = dwo.astype(BF).reshape(dwo_ref.shape)
    for k, ref in enumerate(outs):
        ref[:chunk, :] = (mine_ref[row ^ k].astype(F32) + got_ref[row ^ k].astype(F32)).astype(BF)
        ref[chunk:, :] = dwo_ref[row ^ k]


def add_all(refs):
    return functools.reduce(lambda a, b: a + b, [ref[...].astype(F32) for ref in refs])


def weights_kernel(n_row, n_col, normed_ref, mask_ref, *refs):
    col_refs, row_refs = refs[:n_col][::-1], refs[n_col : n_row + n_col][::-1]
    pay_ref, parts_ref, couple_ref, spread = refs[n_row + n_col :]
    q, seqs, _ = normed_ref.shape
    chunk = q * PROJ
    mask = own_mask(mask_ref, seqs)
    g_left = add_all([ref.at[:chunk, :] for ref in col_refs])
    g_right = add_all([ref.at[:chunk, :] for ref in row_refs])
    pay_ref[4 * PROJ :, :] = add_all([ref.at[chunk:, :] for ref in row_refs]).astype(BF)
    spread[...] = (g_right.reshape(PROJ, q, seqs) * mask[None]).reshape(chunk, seqs)
    total = jnp.zeros((4 * PROJ, ALIGN), F32)
    for i in range(q):
        left = g_left[i * PROJ : (i + 1) * PROJ] * mask[i : i + 1, :]
        g = jnp.concatenate([left, spread[pl.ds(i, PROJ, stride=q), :]], axis=0)
        high = g.astype(BF).astype(F32)
        parts = jnp.concatenate([high, g - high], axis=0).astype(BF)
        parts_ref[i] = parts
        total = total + dot(parts, normed_ref[i], NN)
    d_weights = total[: 2 * PROJ] + total[2 * PROJ :]
    pay_ref[: 2 * PROJ, :] = d_weights[:, :128].astype(BF)
    pay_ref[2 * PROJ : 4 * PROJ, :] = d_weights[:, 128:].astype(BF)
    for k, ref in enumerate(col_refs):
        couple_ref[lax.axis_index("col") ^ k] = ref[chunk:, :]


def hold_kernel(right_ref, left_ref, w_ref, right_out, left_out, wp_ref, wf):
    right_out[...] = right_ref[...]
    left_out[...] = left_ref[...]
    wf[...] = w_ref[...].astype(F32)
    for e in range(PROJ):
        wp_ref[e * PROJ : (e + 1) * PROJ, :] = wf[pl.ds(e, PROJ, stride=PROJ), :].astype(BF)


def input_kernel(x_ref, wl_ref, wr_ref, parts_ref, dx_ref, token_ref, rows):
    q, _, seqs = parts_ref.shape
    weights = jnp.concatenate([wl_ref[...], wr_ref[...]] * 2, axis=0)
    for i in range(q):
        d_rows = dot(parts_ref[i], weights, TN)
        rows[0, pl.ds(i, seqs, stride=q), :] = d_rows[:, :128]
        rows[1, pl.ds(i, seqs, stride=q), :] = d_rows[:, 128:]
    xhat, rstd = normalize(x_ref[...].astype(F32))
    d_normed = strided(rows, slice(None))
    along = jnp.mean(d_normed * xhat, axis=-1, keepdims=True)
    dx = rstd * (d_normed - jnp.mean(d_normed, axis=-1, keepdims=True) - xhat * along)
    dx_ref[...] = dx.astype(BF)
    token_ref[...] = jnp.zeros_like(token_ref)


def place_kernel(q, couple_ref, out_ref, token_ref):
    pieces = [couple_ref[p].astype(F32).reshape(-1, q, CZ) for p in range(couple_ref.shape[0])]
    out_ref[...] = jnp.stack(pieces, axis=1).reshape(-1, CZ).astype(BF)
    token_ref[...] = jnp.zeros_like(token_ref)


def sum_kernel(axis, size, *refs):
    out_ref, held = refs[-2:]
    for k, ref in enumerate(by_partner(refs[:size])):
        held[lax.axis_index(axis) ^ k] = ref[...]
    out_ref[...] = add_all([held.at[k] for k in range(size)]).astype(BF)


def join_kernel(axis, size, *refs):
    ins = refs[:size][::-1]
    out_ref, sums, runs = refs[-3:]
    head = 4 * PROJ
    rows = ins[0].shape[0] - head
    for k, ref in enumerate(ins):
        place = lax.axis_index(axis) ^ k
        sums[place] = ref[:head, :]
        runs[pl.ds(pl.multiple_of(place * rows, rows), rows), :] = ref[head:, :].astype(F32)
    out_ref[:head, :] = add_all([sums.at[k] for k in range(size)]).astype(BF)
    out_ref[head:, :] = runs[...].astype(BF)


def total_kernel(mine_ref, theirs_ref, first_ref, second_ref, dwo_ref):
    head = 4 * PROJ
    seq = lax.axis_index("seq")
    for ref, side in ((mine_ref, seq), (theirs_ref, 1 - seq)):
        start = pl.multiple_of(side * (OUTER // 2), OUTER // 2)
        dwo_ref[pl.ds(start, OUTER // 2), :] = ref[head:, :].astype(F32)
    total = mine_ref[:head, :].astype(F32) + theirs_ref[:head, :].astype(F32)
    first_ref[:, :128] = total[:PROJ]
    first_ref[:, 128:] = total[2 * PROJ : 3 * PROJ]
    second_ref[:, :128] = total[PROJ : 2 * PROJ]
    second_ref[:, 128:] = total[3 * PROJ :]


def params(mib):
    return pltpu.CompilerParams(vmem_limit_bytes=mib * 1024 * 1024)


def shape(*dims, dtype=BF):
    return jax.ShapeDtypeStruct(dims, dtype)


def call(kernel, name, inputs, outputs, scratch=(), hbm_in=0, hbm_out=0, sems=0, mib=None, cost=None):
    def specs(count, hbm):
        return [pl.BlockSpec(memory_space=pltpu.HBM if k < hbm else pltpu.VMEM) for k in range(count)]

    held = sum(2 * math.prod(dims) for dims, _ in scratch)
    buffers = [pltpu.VMEM(dims, dtype) for dims, dtype in scratch]
    if sems:
        buffers.append(pltpu.SemaphoreType.DMA((sems,)))
    return pl.pallas_call(
        kernel,
        out_shape=outputs,
        in_specs=specs(len(inputs), hbm_in),
        out_specs=tuple(specs(len(outputs), hbm_out)),
        scratch_shapes=buffers,
        compiler_params=params(mib or 16 + 2 * held // 1024**2),
        cost_estimate=cost and pl.CostEstimate(flops=cost[0], bytes_accessed=cost[1], transcendentals=0),
        name=name,
    )(*inputs)


def local(n_row, n_col, n_seq, x, occupancy, first, second, couple, adjoint):
    seqs, q, _ = x.shape
    rows_i, rows_j, _ = adjoint.shape
    half = n_col // n_seq
    chunk = q * PROJ
    depth = seqs * n_seq
    pairs = rows_i * q
    flat = x.reshape(seqs * q, ALIGN)
    mask = occupancy.T
    wl, wr = first.T, second.T

    right, *lefts = call(
        project_kernel,
        "project",
        (flat, mask, wl, wr, adjoint.reshape(rows_i * rows_j, CZ)),
        (
            shape(chunk + PAD, seqs),
            *[shape(chunk + PAD + pairs, seqs)] * n_col,
        ),
        [
            ((seqs * q, ALIGN), BF),
            ((q, depth), jnp.int32),
            ((PROJ, ALIGN), BF),
            ((PROJ, ALIGN), BF),
            ((rows_i * rows_j, CZ), BF),
            ((chunk + PAD, seqs), BF),
            ((chunk + PAD, seqs), BF),
            ((n_col, pairs, CZ), BF),
            ((2, seqs * q, ALIGN // 2), F32),
            ((chunk, seqs), F32),
        ],
        hbm_in=5,
        hbm_out=1 + n_col,
        sems=6 + 2 * n_col,
        mib=60,
    )

    def partner(value, axis, k):
        size = {"row": n_row, "col": n_col, "seq": n_seq}[axis]
        return lax.ppermute(value, axis, [(d, d ^ k) for d in range(size)])

    def spread(values, axis):
        return [values[0]] + [partner(values[k], axis, k) for k in range(1, len(values))]

    held, left, wp = call(
        hold_kernel,
        "hold",
        (right, lefts[0], couple),
        (shape(*right.shape), shape(*lefts[0].shape), shape(OUTER, CZ)),
        [((OUTER, CZ), F32)],
        cost=(2**20, 2**20),
    )
    rights = [held] + spread([right] * n_row, "row")[1:]
    lefts = [left] + spread(lefts, "col")[1:]
    normed, ready = call(
        norm_kernel,
        "norm",
        (flat,),
        (shape(q, seqs, ALIGN), shape(8, CZ, dtype=F32)),
        [((2, seqs * q, ALIGN // 2), F32)],
        cost=(2**28, 2**21),
    )
    count = n_row + half
    mine, theirs, mask_right, mask_left, adjoints = call(
        functools.partial(pack_kernel, n_row),
        "pack",
        (ready, *lefts[::-1], *rights),
        (
            shape(count, chunk, seqs),
            shape(count, chunk, seqs),
            shape(rows_j, depth, dtype=F32),
            shape(rows_i, depth, dtype=F32),
            shape(n_col, pairs, CZ),
        ),
        [((n_col, chunk, seqs), BF), ((n_col, q, depth), F32)],
    )
    theirs = partner(theirs, "seq", 1)
    dd, scaled, recip, rt_mine = call(
        back_kernel,
        "back",
        (wp, mask_right, mask_left, adjoints, mine),
        (
            shape(PROJ * rows_j, rows_i * PROJ),
            shape(CZ, rows_i * rows_j),
            shape(rows_i * rows_j, CZ, dtype=F32),
            shape(PROJ * rows_j, seqs),
        ),
        [((rows_i * rows_j, OUTER), F32)],
        cost=(2**30, 2**23),
    )
    rt, left_mine, left_theirs = call(
        left_kernel,
        "left",
        (rt_mine, theirs, dd),
        (shape(PROJ * rows_j, depth), shape(half, chunk, seqs), shape(half, chunk, seqs)),
        [((2, half, chunk, seqs), BF)],
        cost=(2**30, 2**23),
    )
    got = partner(left_theirs, "seq", 1)
    parts = n_row + OUTER // 2 // chunk
    right_mine, right_theirs, pieces = call(
        pair_kernel,
        "pair",
        (rt, wp, dd, scaled, recip, mine, theirs),
        (
            shape(parts, chunk, seqs),
            shape(parts, chunk, seqs),
            shape(n_col, pairs, CZ),
        ),
        [
            ((rows_i * PROJ, depth), BF),
            ((OUTER, CZ), F32),
            ((rows_i * rows_j, OUTER), BF),
            ((2, parts, chunk, seqs), BF),
        ],
        cost=(2**30, 2**23),
    )
    piece = OUTER // 2 // n_row
    right_theirs, *lefts = call(
        merge_left_kernel,
        "merge_left",
        (left_mine, got, pieces, right_theirs),
        [shape(*right_theirs.shape)] + [shape(chunk + pairs, seqs)] * n_col,
        [((n_col, chunk, seqs), BF)],
    )
    lefts = spread(lefts, "col")
    rights = call(
        merge_right_kernel,
        "merge_right",
        (right_mine, partner(right_theirs, "seq", 1)),
        [shape(chunk + piece, seqs)] * n_row,
        [((n_row, piece, CZ), BF)],
    )
    rights = spread(rights, "row")
    pay, parts, pieces = call(
        functools.partial(weights_kernel, n_row, n_col),
        "weights",
        (normed, mask, *lefts[::-1], *rights[::-1]),
        (
            shape(4 * PROJ + piece, CZ),
            shape(q, 4 * PROJ, seqs),
            shape(n_col, pairs, CZ),
        ),
        [((chunk, seqs), F32)],
    )
    dx, token = call(
        input_kernel,
        "input",
        (flat, wl, wr, parts),
        (shape(seqs * q, ALIGN), shape(8, CZ, dtype=F32)),
        [((2, seqs * q, ALIGN // 2), F32)],
        cost=(2**28, 2**21),
    )
    increment, placed = call(
        functools.partial(place_kernel, q),
        "place",
        (pieces,),
        (shape(rows_i * rows_j, CZ), shape(8, CZ, dtype=F32)),
        cost=(2**20, 2**20),
    )

    (pay,) = call(
        functools.partial(sum_kernel, "col", n_col),
        "sum",
        (*sent_order(spread([pay] * n_col, "col")), token),
        (shape(*pay.shape),),
        [((n_col, *pay.shape), BF)],
    )
    (pay,) = call(
        functools.partial(join_kernel, "row", n_row),
        "join",
        (*spread([pay] * n_row, "row")[::-1], placed),
        (shape(4 * PROJ + n_row * piece, CZ),),
        [((n_row, 4 * PROJ, CZ), BF), ((n_row * piece, CZ), F32)],
    )
    d_first, d_second, d_couple = call(
        total_kernel,
        "total",
        (pay, partner(pay, "seq", 1)),
        (shape(PROJ, ALIGN, dtype=F32), shape(PROJ, ALIGN, dtype=F32), shape(OUTER, CZ, dtype=F32)),
    )
    return (
        increment.reshape(rows_i, rows_j, CZ),
        dx.reshape(seqs, q, ALIGN),
        d_first.T,
        d_second.T,
        d_couple,
    )


def solution(mesh):
    sizes = [mesh.shape[name] for name in AXES]
    placed = (
        P("seq", ("row", "col"), None),
        P(None, ("row", "col")),
        P(),
        P(),
        P(),
        P(("row", "seq"), "col", None),
    )
    return jax.shard_map(
        functools.partial(local, *sizes),
        mesh=mesh,
        in_specs=placed,
        out_specs=(P(("row", "seq"), "col", None), P("seq", ("row", "col"), None), P(), P(), P()),
        check_vma=False,
    )
```

time: 595 us -> 53.6 us (0.09)
  waiting for transfers between devices: 432 us -> 15.4 us
  blocking collectives: 48.9 us -> 0 us
  local copies, waits for them, and re-layouts: 50.5 us -> 1.8 us
  matrix products: 38.3 us -> 0 us
  starting transfers between devices: 0.43 us -> 24.3 us
  between operations: 14.4 us -> 0.78 us
  Pallas kernels: 0 us -> 11.2 us
  other arithmetic: 9.3 us -> 0 us
    psum x5 -> x0, waiting for transfers between devices: 429 us -> none  [the longest x2 254 us: local(): lax.psum((first_factor_adjoint, second_factor_adjoint, d_wo), ('row', 'co...]
    dot_general x13 -> x0, matrix products: 38.3 us -> none  [the longest x1 8.69 us: local(): jnp.einsum('sic,sje->ijce', lblock, right_cols, preferred_element_type=jn...]
    all_gather x3 -> x0, blocking collectives: 32.8 us -> none  [the longest x1 17.4 us: local(): lax.all_gather(stacked, 'col', axis=1, tiled=True)]
    ppermute x0 -> x22, starting transfers between devices: none -> 24.3 us  [partner(): return lax.ppermute(value, axis, [(d, d ^ k) for d in range(size)])]
    reshape x2 -> x0, local copies, waits for them, and re-layouts: 21.6 us -> none  [the longest x1 13.7 us: local(): outer.reshape(half * lax.axis_size('seq'), block, OUTER)]
    transpose x1 -> x0, local copies, waits for them, and re-layouts: 17.5 us -> none  [local(): jnp.einsum('sic,sje->ijce', lblock, right_cols, preferred_element_type=jn...]
    psum x1 -> x0, blocking collectives: 16.1 us -> none  [broadcast(): return lax.psum(jnp.where(mine, value, jnp.zeros_like(value)), axis)]
    ppermute x0 -> x22, waiting for transfers between devices: none -> 15.4 us  [partner(): return lax.ppermute(value, axis, [(d, d ^ k) for d in range(size)])]
  transfers between devices with their start and end apart: 6 -> 22, of which waited for: 5 -> 15; matrix products, arithmetic and copies ran while one was open for 14% -> 0% of each run, Pallas kernels for 0% -> 12%
where the time goes in v1:
time: 53.6 us; the launch traced here: 53.4 us
  starting transfers between devices  24.3 us (45%)
  waiting for transfers between devices  15.4 us (29%)
  Pallas kernels  11.2 us (21%)
  local copies, waits for them, and re-layouts  1.8 us (3%)
  between operations  0.78 us (1%)
    ppermute x22, starting transfers between devices, partner(): return lax.ppermute(value, axis, [(d, d ^ k) for d in range(size)])  24.3 us
    ppermute x22, waiting for transfers between devices, partner(): return lax.ppermute(value, axis, [(d, d ^ k) for d in range(size)])  15.4 us
    pallas_call x15, Pallas kernels, call(): pl.pallas_call(kernel, out_shape=outputs, in_specs=specs(len(inputs), hbm...  11.2 us
    unnamed x14, local copies, waits for them, and re-layouts  1.8 us
  transfers between devices with their start and end apart: 22, of which 15 were waited for; matrix products, arithmetic and copies ran while one was open for 0% of the time, Pallas kernels for 12%

profile of v1, /device:TPU:0, one launch (start us, length us, event | category | flops | bytes accessed | tf_op | source)
XLA Modules:
  0.0 53.4 jit_solution(10421848422215809813)
XLA Ops:
  0.7 2.7 %project.1 = (bf16[272,128]{1,0:T(8,128)(2,1)}, bf16[400,128]{1,0:T(8,128)(2,1)}, bf16[400,128]{1,0:T(8,128)(2,1)}, bf16[400,128]{1,0:T(8,128)(2,1)}, bf16[400,128]{1,0:T(8,128)(2,1)}) custom-call(bf16[1024,256]{1,0:T(8,128)(2,1)} %bitcast.9, s32[8,256]{1,0:T(8,128)} %bitcast.12, bf16[32,256]{1,0:T(8,128)(2,1)} %bitcast.14, bf16[32,256]{1,0:T(8,128)(2,1)} %bitcast.16, ...), custom_call_target="tpu_custom_call" | custom-call | tf_op jit(solution)/shard_map/project/pallas_call | solution.py:383
  3.4 3.0 %collective-permute-start.3 = (bf16[272,128]{1,0:T(8,128)(2,1)}, bf16[272,128]{1,0:T(8,128)(2,1)S(1)}, u32[]{:S(2)}, u32[]{:S(2)}) collective-permute-start(bf16[272,128]{1,0:T(8,128)(2,1)} %get-tuple-element.50.right_ref), channel_id=1, source_target_pairs={{0,8},{8,0},{16,24},{24,16},{1,9},{9,1},{17,25},{25,17},{2,10},{10... | collective-permute-start | bytes 208904 | tf_op jit(solution)/shard_map/ppermute | solution.py:434
  6.4 3.6 %collective-permute-start = (bf16[400,128]{1,0:T(8,128)(2,1)}, bf16[400,128]{1,0:T(8,128)(2,1)S(1)}, u32[]{:S(2)}, u32[]{:S(2)}) collective-permute-start(bf16[400,128]{1,0:T(8,128)(2,1)} %get-tuple-element.54), channel_id=1, source_target_pairs={{0,6},{2,4},{4,2},{6,0},{1,7},{3,5},{5,3},{7,1},{8,14},{10,12},{12... | collective-permute-start | bytes 307208 | tf_op jit(solution)/shard_map/ppermute | solution.py:434
  10.0 0.8 %collective-permute-start.2 = (bf16[400,128]{1,0:T(8,128)(2,1)}, bf16[400,128]{1,0:T(8,128)(2,1)S(1)}, u32[]{:S(2)}, u32[]{:S(2)}) collective-permute-start(bf16[400,128]{1,0:T(8,128)(2,1)} %get-tuple-element.56), channel_id=1, source_target_pairs={{0,2},{2,0},{4,6},{6,4},{1,3},{3,1},{5,7},{7,5},{8,10},{10,8},{12,... | collective-permute-start | bytes 307208 | tf_op jit(solution)/shard_map/ppermute | solution.py:434
  10.7 1.5 %collective-permute-start.4 = (bf16[272,128]{1,0:T(8,128)(2,1)}, bf16[272,128]{1,0:T(8,128)(2,1)S(1)}, u32[]{:S(2)}, u32[]{:S(2)}) collective-permute-start(bf16[272,128]{1,0:T(8,128)(2,1)} %get-tuple-element.50.right_ref), channel_id=1, source_target_pairs={{0,16},{8,24},{16,0},{24,8},{1,17},{9,25},{17,1},{25,9},{2,18},{10... | collective-permute-start | bytes 208904 | tf_op jit(solution)/shard_map/ppermute | solution.py:434
  12.3 0.3 collective-permute-start.5
  12.5 0.9 %copy-done.2 = bf16[400,128]{1,0:T(8,128)(2,1)S(1)} copy-done((bf16[400,128]{1,0:T(8,128)(2,1)S(1)}, bf16[400,128]{1,0:T(8,128)(2,1)}, u32[]{:S(2)}) %copy-start.2) | copy-done | bytes 102424
  13.4 0.9 %copy-done.3 = bf16[272,128]{1,0:T(8,128)(2,1)S(1)} copy-done((bf16[272,128]{1,0:T(8,128)(2,1)S(1)}, bf16[272,128]{1,0:T(8,128)(2,1)}, u32[]{:S(2)}) %copy-start.3) | copy-done | bytes 69656
  14.3 0.3 hold.1
  14.7 0.5 norm.1
  15.2 0.8 %collective-permute-done.4.refs_6_ = bf16[272,128]{1,0:T(8,128)(2,1)S(1)} collective-permute-done((bf16[272,128]{1,0:T(8,128)(2,1)}, bf16[272,128]{1,0:T(8,128)(2,1)S(1)}, u32[]{:S(2)}, u32[]{:S(2)}) %collective-permute-start.4) | collective-permute-done | bytes 69664 | tf_op jit(solution)/shard_map/ppermute | solution.py:434
  16.0 1.7 %collective-permute-done.5.refs_7_ = bf16[272,128]{1,0:T(8,128)(2,1)S(1)} collective-permute-done((bf16[272,128]{1,0:T(8,128)(2,1)}, bf16[272,128]{1,0:T(8,128)(2,1)S(1)}, u32[]{:S(2)}, u32[]{:S(2)}) %collective-permute-start.5) | collective-permute-done | bytes 69664 | tf_op jit(solution)/shard_map/ppermute | solution.py:434
  17.7 0.8 %collective-permute-done.1.refs_1_ = bf16[400,128]{1,0:T(8,128)(2,1)S(1)} collective-permute-done((bf16[400,128]{1,0:T(8,128)(2,1)}, bf16[400,128]{1,0:T(8,128)(2,1)S(1)}, u32[]{:S(2)}, u32[]{:S(2)}) %collective-permute-start.1) | collective-permute-done | bytes 102432 | tf_op jit(solution)/shard_map/ppermute | solution.py:434
  18.5 0.1 pack.1
  18.6 0.1 collective-permute-start.6
  18.7 0.9 %back.1 = (bf16[1024,512]{1,0:T(8,128)(2,1)S(1)}, bf16[128,512]{1,0:T(8,128)(2,1)S(1)}, f32[512,128]{1,0:T(8,128)S(1)}, bf16[1024,128]{1,0:T(8,128)(2,1)S(1)}) custom-call(bf16[1024,128]{1,0:T(8,128)(2,1)S(1)} %get-tuple-element.52.wp, f32[32,256]{1,0:T(8,128)S(1)} %get-tuple-element.59.mr, f32[16,256]{1,0:T(8,128)S(1)} %get-tuple-element.60.ml, ...), custom_call_target="tpu_custom_call" | custom-call | flops 1073741824 | bytes 8388608 | tf_op jit(solution)/shard_map/back/pallas_call | solution.py:383
  19.7 0.8 %collective-permute-done.6.theirs = bf16[6,256,128]{2,1,0:T(8,128)(2,1)S(1)} collective-permute-done((bf16[6,256,128]{2,1,0:T(8,128)(2,1)S(1)}, bf16[6,256,128]{2,1,0:T(8,128)(2,1)S(1)}, u32[]{:S(2)}, u32[]{:S(2)}) %collective-permute-start.6) | collective-permute-done | bytes 393248 | tf_op jit(solution)/shard_map/ppermute | solution.py:434
  20.4 0.7 %left.1 = (bf16[1024,256]{1,0:T(8,128)(2,1)S(1)}, bf16[2,256,128]{2,1,0:T(8,128)(2,1)S(1)}, bf16[2,256,128]{2,1,0:T(8,128)(2,1)S(1)}) custom-call(bf16[1024,128]{1,0:T(8,128)(2,1)S(1)} %get-tuple-element.63.rt_mine, bf16[6,256,128]{2,1,0:T(8,128)(2,1)S(1)} %collective-permute-done.6.theirs, bf16[1024,512]{1,0:T(8,128)(2,1)S(1)} %get-tuple-element.65.dd), custom_call_target="tpu_custom_call" | custom-call | flops 1073741824 | bytes 8388608 | tf_op jit(solution)/shard_map/left/pallas_call | solution.py:383
  21.1 0.2 collective-permute-start.7
  21.3 2.0 %pair.1 = (bf16[6,256,128]{2,1,0:T(8,128)(2,1)S(1)}, bf16[6,256,128]{2,1,0:T(8,128)(2,1)S(1)}, bf16[4,128,128]{2,1,0:T(8,128)(2,1)S(1)}) custom-call(bf16[1024,256]{1,0:T(8,128)(2,1)S(1)} %get-tuple-element.68.rt, bf16[1024,128]{1,0:T(8,128)(2,1)S(1)} %get-tuple-element.52.wp, bf16[1024,512]{1,0:T(8,128)(2,1)S(1)} %get-tuple-element.65.dd, ...), custom_call_target="tpu_custom_call" | custom-call | flops 1073741824 | bytes 8388608 | tf_op jit(solution)/shard_map/pair/pallas_call | solution.py:383
  23.3 0.1 merge_left.1
  23.4 0.4 collective-permute-start.11
  23.8 2.8 %collective-permute-start.8 = (bf16[384,128]{1,0:T(8,128)(2,1)S(1)}, bf16[384,128]{1,0:T(8,128)(2,1)S(1)}, u32[]{:S(2)}, u32[]{:S(2)}) collective-permute-start(bf16[384,128]{1,0:T(8,128)(2,1)S(1)} %get-tuple-element.73), channel_id=1, source_target_pairs={{0,6},{2,4},{4,2},{6,0},{1,7},{3,5},{5,3},{7,1},{8,14},{10,12},{12... | collective-permute-start | bytes 294920 | tf_op jit(solution)/shard_map/ppermute | solution.py:434
  26.6 1.6 %collective-permute-start.10 = (bf16[384,128]{1,0:T(8,128)(2,1)S(1)}, bf16[384,128]{1,0:T(8,128)(2,1)S(1)}, u32[]{:S(2)}, u32[]{:S(2)}) collective-permute-start(bf16[384,128]{1,0:T(8,128)(2,1)S(1)} %get-tuple-element.75), channel_id=1, source_target_pairs={{0,2},{2,0},{4,6},{6,4},{1,3},{3,1},{5,7},{7,5},{8,10},{10,8},{12,... | collective-permute-start | bytes 294920 | tf_op jit(solution)/shard_map/ppermute | solution.py:434
  28.2 0.1 merge_right.1
  28.4 1.6 %collective-permute-start.12 = (bf16[384,128]{1,0:T(8,128)(2,1)S(1)}, bf16[384,128]{1,0:T(8,128)(2,1)S(1)}, u32[]{:S(2)}, u32[]{:S(2)}) collective-permute-start(bf16[384,128]{1,0:T(8,128)(2,1)S(1)} %get-tuple-element.79), channel_id=1, source_target_pairs={{0,24},{8,16},{16,8},{24,0},{1,25},{9,17},{17,9},{25,1},{2,26},{10... | collective-permute-start | bytes 294920 | tf_op jit(solution)/shard_map/ppermute | solution.py:434
  29.9 0.5 collective-permute-start.13
  30.4 1.0 %collective-permute-done.8.refs_0_ = bf16[384,128]{1,0:T(8,128)(2,1)S(1)} collective-permute-done((bf16[384,128]{1,0:T(8,128)(2,1)S(1)}, bf16[384,128]{1,0:T(8,128)(2,1)S(1)}, u32[]{:S(2)}, u32[]{:S(2)}) %collective-permute-start.8) | collective-permute-done | bytes 98336 | tf_op jit(solution)/shard_map/ppermute | solution.py:434
  31.4 0.5 %collective-permute-start.14 = (bf16[384,128]{1,0:T(8,128)(2,1)S(1)}, bf16[384,128]{1,0:T(8,128)(2,1)S(1)}, u32[]{:S(2)}, u32[]{:S(2)}) collective-permute-start(bf16[384,128]{1,0:T(8,128)(2,1)S(1)} %get-tuple-element.81), channel_id=1, source_target_pairs={{0,8},{8,0},{16,24},{24,16},{1,9},{9,1},{17,25},{25,17},{2,10},{10... | collective-permute-start | bytes 294920 | tf_op jit(solution)/shard_map/ppermute | solution.py:434
  31.9 3.0 %collective-permute-done.9.refs_1_ = bf16[384,128]{1,0:T(8,128)(2,1)S(1)} collective-permute-done((bf16[384,128]{1,0:T(8,128)(2,1)S(1)}, bf16[384,128]{1,0:T(8,128)(2,1)S(1)}, u32[]{:S(2)}, u32[]{:S(2)}) %collective-permute-start.9) | collective-permute-done | bytes 98336 | tf_op jit(solution)/shard_map/ppermute | solution.py:434
  34.9 0.5 %collective-permute-done.13.refs_5_ = bf16[384,128]{1,0:T(8,128)(2,1)S(1)} collective-permute-done((bf16[384,128]{1,0:T(8,128)(2,1)S(1)}, bf16[384,128]{1,0:T(8,128)(2,1)S(1)}, u32[]{:S(2)}, u32[]{:S(2)}) %collective-permute-start.13) | collective-permute-done | bytes 98336 | tf_op jit(solution)/shard_map/ppermute | solution.py:434
  35.4 0.6 %collective-permute-done.14.refs_6_ = bf16[384,128]{1,0:T(8,128)(2,1)S(1)} collective-permute-done((bf16[384,128]{1,0:T(8,128)(2,1)S(1)}, bf16[384,128]{1,0:T(8,128)(2,1)S(1)}, u32[]{:S(2)}, u32[]{:S(2)}) %collective-permute-start.14) | collective-permute-done | bytes 98336 | tf_op jit(solution)/shard_map/ppermute | solution.py:434
  36.0 0.3 weights.1
  36.4 1.1 %collective-permute-start.15 = (bf16[256,128]{1,0:T(8,128)(2,1)S(1)}, bf16[256,128]{1,0:T(8,128)(2,1)S(1)}, u32[]{:S(2)}, u32[]{:S(2)}) collective-permute-start(bf16[256,128]{1,0:T(8,128)(2,1)S(1)} %get-tuple-element.87.refs_2_), channel_id=1, source_target_pairs={{0,4},{2,6},{4,0},{6,2},{1,5},{3,7},{5,1},{7,3},{8,12},{10,14},{12... | collective-permute-start | bytes 196616 | tf_op jit(solution)/shard_map/ppermute | solution.py:434
  37.5 2.6 %collective-permute-start.16 = (bf16[256,128]{1,0:T(8,128)(2,1)S(1)}, bf16[256,128]{1,0:T(8,128)(2,1)S(1)}, u32[]{:S(2)}, u32[]{:S(2)}) collective-permute-start(bf16[256,128]{1,0:T(8,128)(2,1)S(1)} %get-tuple-element.87.refs_2_), channel_id=1, source_target_pairs={{0,6},{2,4},{4,2},{6,0},{1,7},{3,5},{5,3},{7,1},{8,14},{10,12},{12... | collective-permute-start | bytes 196616 | tf_op jit(solution)/shard_map/ppermute | solution.py:434
  40.1 1.7 %input.1 = (bf16[1024,256]{1,0:T(8,128)(2,1)}, f32[8,128]{1,0:T(8,128)S(1)}) custom-call(bf16[1024,256]{1,0:T(8,128)(2,1)S(1)} %bitcast.11, bf16[32,256]{1,0:T(8,128)(2,1)S(1)} %bitcast.15, bf16[32,256]{1,0:T(8,128)(2,1)S(1)} %bitcast.17, bf16[8,128,128]{2,1,0:T(8,128)(2,1)S(1)} %get-tuple-element.85.parts_ref), custom_call_target="tpu_custom_call" | custom-call | flops 268435456 | bytes 2097152 | tf_op jit(solution)/shard_map/input/pallas_call | solution.py:383
  41.8 1.5 %collective-permute-done.15.refs_0_ = bf16[256,128]{1,0:T(8,128)(2,1)S(1)} collective-permute-done((bf16[256,128]{1,0:T(8,128)(2,1)S(1)}, bf16[256,128]{1,0:T(8,128)(2,1)S(1)}, u32[]{:S(2)}, u32[]{:S(2)}) %collective-permute-start.15) | collective-permute-done | bytes 65568 | tf_op jit(solution)/shard_map/ppermute | solution.py:434
  43.3 0.8 %collective-permute-done.16.refs_1_ = bf16[256,128]{1,0:T(8,128)(2,1)S(1)} collective-permute-done((bf16[256,128]{1,0:T(8,128)(2,1)S(1)}, bf16[256,128]{1,0:T(8,128)(2,1)S(1)}, u32[]{:S(2)}, u32[]{:S(2)}) %collective-permute-start.16) | collective-permute-done | bytes 65568 | tf_op jit(solution)/shard_map/ppermute | solution.py:434
  44.1 0.7 %collective-permute-done.17.refs_3_ = bf16[256,128]{1,0:T(8,128)(2,1)S(1)} collective-permute-done((bf16[256,128]{1,0:T(8,128)(2,1)S(1)}, bf16[256,128]{1,0:T(8,128)(2,1)S(1)}, u32[]{:S(2)}, u32[]{:S(2)}) %collective-permute-start.17) | collective-permute-done | bytes 65568 | tf_op jit(solution)/shard_map/ppermute | solution.py:434
  44.8 1.2 %collective-permute-start.18 = (bf16[256,128]{1,0:T(8,128)(2,1)S(1)}, bf16[256,128]{1,0:T(8,128)(2,1)S(1)}, u32[]{:S(2)}, u32[]{:S(2)}) collective-permute-start(bf16[256,128]{1,0:T(8,128)(2,1)S(1)} %sum.1.refs_3_), channel_id=1, source_target_pairs={{0,24},{8,16},{16,8},{24,0},{1,25},{9,17},{17,9},{25,1},{2,26},{10... | collective-permute-start | bytes 196616 | tf_op jit(solution)/shard_map/ppermute | solution.py:434
  46.0 0.8 %collective-permute-start.19 = (bf16[256,128]{1,0:T(8,128)(2,1)S(1)}, bf16[256,128]{1,0:T(8,128)(2,1)S(1)}, u32[]{:S(2)}, u32[]{:S(2)}) collective-permute-start(bf16[256,128]{1,0:T(8,128)(2,1)S(1)} %sum.1.refs_3_), channel_id=1, source_target_pairs={{0,16},{8,24},{16,0},{24,8},{1,17},{9,25},{17,1},{25,9},{2,18},{10... | collective-permute-start | bytes 196616 | tf_op jit(solution)/shard_map/ppermute | solution.py:434
  46.8 1.6 %collective-permute-start.20 = (bf16[256,128]{1,0:T(8,128)(2,1)S(1)}, bf16[256,128]{1,0:T(8,128)(2,1)S(1)}, u32[]{:S(2)}, u32[]{:S(2)}) collective-permute-start(bf16[256,128]{1,0:T(8,128)(2,1)S(1)} %sum.1.refs_3_), channel_id=1, source_target_pairs={{0,8},{8,0},{16,24},{24,16},{1,9},{9,1},{17,25},{25,17},{2,10},{10... | collective-permute-start | bytes 196616 | tf_op jit(solution)/shard_map/ppermute | solution.py:434
  48.4 0.7 %place.1 = (bf16[512,128]{1,0:T(8,128)(2,1)}, f32[8,128]{1,0:T(8,128)S(1)}) custom-call(bf16[4,128,128]{2,1,0:T(8,128)(2,1)S(1)} %get-tuple-element.83.couple_ref), custom_call_target="tpu_custom_call" | custom-call | flops 1048576 | bytes 1048576 | tf_op jit(solution)/shard_map/place/pallas_call | solution.py:383
  49.1 1.0 %collective-permute-done.18.refs_0_ = bf16[256,128]{1,0:T(8,128)(2,1)S(1)} collective-permute-done((bf16[256,128]{1,0:T(8,128)(2,1)S(1)}, bf16[256,128]{1,0:T(8,128)(2,1)S(1)}, u32[]{:S(2)}, u32[]{:S(2)}) %collective-permute-start.18) | collective-permute-done | bytes 65568 | tf_op jit(solution)/shard_map/ppermute | solution.py:434
  50.1 0.7 %collective-permute-done.19.refs_1_ = bf16[256,128]{1,0:T(8,128)(2,1)S(1)} collective-permute-done((bf16[256,128]{1,0:T(8,128)(2,1)S(1)}, bf16[256,128]{1,0:T(8,128)(2,1)S(1)}, u32[]{:S(2)}, u32[]{:S(2)}) %collective-permute-start.19) | collective-permute-done | bytes 65568 | tf_op jit(solution)/shard_map/ppermute | solution.py:434
  50.8 0.3 collective-permute-done.20.refs_2_
  51.2 1.4 %collective-permute-done.21.theirs_ref = bf16[640,128]{1,0:T(8,128)(2,1)S(1)} collective-permute-done((bf16[640,128]{1,0:T(8,128)(2,1)S(1)}, bf16[640,128]{1,0:T(8,128)(2,1)S(1)}, u32[]{:S(2)}, u32[]{:S(2)}) %collective-permute-start.21) | collective-permute-done | bytes 163872 | tf_op jit(solution)/shard_map/ppermute | solution.py:434
  52.6 0.8 %total.1 = (f32[32,256]{1,0:T(8,128)}, f32[32,256]{1,0:T(8,128)}, f32[1024,128]{1,0:T(8,128)}) custom-call(bf16[640,128]{1,0:T(8,128)(2,1)S(1)} %join.1.mine_ref, bf16[640,128]{1,0:T(8,128)(2,1)S(1)} %collective-permute-done.21.theirs_ref), custom_call_target="tpu_custom_call" | custom-call | tf_op jit(solution)/shard_map/total/pallas_call | solution.py:383
  (25 shorter events, 0.3 us)
Async XLA Ops:
  0.6 11.9 %copy-start.1 = (bf16[1024,128]{1,0:T(8,128)(2,1)S(1)}, bf16[1024,128]{1,0:T(8,128)(2,1)}, u32[]{:S(2)}) copy-start(bf16[1024,128]{1,0:T(8,128)(2,1)} %w_ref.1) | copy-start | bytes 786436
  0.6 14.0 %copy-start = (bf16[128,8,256]{2,1,0:T(8,128)(2,1)S(1)}, bf16[128,8,256]{2,1,0:T(8,128)(2,1)}, u32[]{:S(2)}) copy-start(bf16[128,8,256]{2,1,0:T(8,128)(2,1)} %param.6) | copy-start | bytes 1572868
  3.4 8.9 %collective-permute-start.3 = (bf16[272,128]{1,0:T(8,128)(2,1)}, bf16[272,128]{1,0:T(8,128)(2,1)S(1)}, u32[]{:S(2)}, u32[]{:S(2)}) collective-permute-start(bf16[272,128]{1,0:T(8,128)(2,1)} %get-tuple-element.50.right_ref), channel_id=1, source_target_pairs={{0,8},{8,0},{16,24},{24,16},{1,9},{9,1},{17,25},{25,17},{2,10},{10... | collective-permute-start | bytes 208904 | tf_op jit(solution)/shard_map/ppermute | solution.py:434
  6.4 11.3 %collective-permute-start = (bf16[400,128]{1,0:T(8,128)(2,1)}, bf16[400,128]{1,0:T(8,128)(2,1)S(1)}, u32[]{:S(2)}, u32[]{:S(2)}) collective-permute-start(bf16[400,128]{1,0:T(8,128)(2,1)} %get-tuple-element.54), channel_id=1, source_target_pairs={{0,6},{2,4},{4,2},{6,0},{1,7},{3,5},{5,3},{7,1},{8,14},{10,12},{12... | collective-permute-start | bytes 307208 | tf_op jit(solution)/shard_map/ppermute | solution.py:434
  10.0 8.5 %collective-permute-start.1 = (bf16[400,128]{1,0:T(8,128)(2,1)}, bf16[400,128]{1,0:T(8,128)(2,1)S(1)}, u32[]{:S(2)}, u32[]{:S(2)}) collective-permute-start(bf16[400,128]{1,0:T(8,128)(2,1)} %get-tuple-element.55), channel_id=1, source_target_pairs={{0,4},{2,6},{4,0},{6,2},{1,5},{3,7},{5,1},{7,3},{8,12},{10,14},{12... | collective-permute-start | bytes 307208 | tf_op jit(solution)/shard_map/ppermute | solution.py:434
  10.0 8.5 %collective-permute-start.2 = (bf16[400,128]{1,0:T(8,128)(2,1)}, bf16[400,128]{1,0:T(8,128)(2,1)S(1)}, u32[]{:S(2)}, u32[]{:S(2)}) collective-permute-start(bf16[400,128]{1,0:T(8,128)(2,1)} %get-tuple-element.56), channel_id=1, source_target_pairs={{0,2},{2,0},{4,6},{6,4},{1,3},{3,1},{5,7},{7,5},{8,10},{10,8},{12,... | collective-permute-start | bytes 307208 | tf_op jit(solution)/shard_map/ppermute | solution.py:434
  10.7 5.2 %collective-permute-start.4 = (bf16[272,128]{1,0:T(8,128)(2,1)}, bf16[272,128]{1,0:T(8,128)(2,1)S(1)}, u32[]{:S(2)}, u32[]{:S(2)}) collective-permute-start(bf16[272,128]{1,0:T(8,128)(2,1)} %get-tuple-element.50.right_ref), channel_id=1, source_target_pairs={{0,16},{8,24},{16,0},{24,8},{1,17},{9,25},{17,1},{25,9},{2,18},{10... | collective-permute-start | bytes 208904 | tf_op jit(solution)/shard_map/ppermute | solution.py:434
  12.3 5.4 %collective-permute-start.5 = (bf16[272,128]{1,0:T(8,128)(2,1)}, bf16[272,128]{1,0:T(8,128)(2,1)S(1)}, u32[]{:S(2)}, u32[]{:S(2)}) collective-permute-start(bf16[272,128]{1,0:T(8,128)(2,1)} %get-tuple-element.50.right_ref), channel_id=1, source_target_pairs={{0,24},{8,16},{16,8},{24,0},{1,25},{9,17},{17,9},{25,1},{2,26},{10... | collective-permute-start | bytes 208904 | tf_op jit(solution)/shard_map/ppermute | solution.py:434
  12.5 0.9 %copy-start.2 = (bf16[400,128]{1,0:T(8,128)(2,1)S(1)}, bf16[400,128]{1,0:T(8,128)(2,1)}, u32[]{:S(2)}) copy-start(bf16[400,128]{1,0:T(8,128)(2,1)} %get-tuple-element.51.left_ref) | copy-start | bytes 307204
  13.4 0.9 %copy-start.3 = (bf16[272,128]{1,0:T(8,128)(2,1)S(1)}, bf16[272,128]{1,0:T(8,128)(2,1)}, u32[]{:S(2)}) copy-start(bf16[272,128]{1,0:T(8,128)(2,1)} %get-tuple-element.50.right_ref) | copy-start | bytes 208900
  18.6 1.8 %collective-permute-start.6 = (bf16[6,256,128]{2,1,0:T(8,128)(2,1)S(1)}, bf16[6,256,128]{2,1,0:T(8,128)(2,1)S(1)}, u32[]{:S(2)}, u32[]{:S(2)}) collective-permute-start(bf16[6,256,128]{2,1,0:T(8,128)(2,1)S(1)} %get-tuple-element.64), channel_id=1, source_target_pairs={{0,1},{1,0},{2,3},{3,2},{4,5},{5,4},{6,7},{7,6},{8,9},{9,8},{10,11... | collective-permute-start | bytes 1179656 | tf_op jit(solution)/shard_map/ppermute | solution.py:434
  21.1 2.2 %collective-permute-start.7 = (bf16[2,256,128]{2,1,0:T(8,128)(2,1)S(1)}, bf16[2,256,128]{2,1,0:T(8,128)(2,1)S(1)}, u32[]{:S(2)}, u32[]{:S(2)}) collective-permute-start(bf16[2,256,128]{2,1,0:T(8,128)(2,1)S(1)} %get-tuple-element.67), channel_id=1, source_target_pairs={{0,1},{1,0},{2,3},{3,2},{4,5},{5,4},{6,7},{7,6},{8,9},{9,8},{10,11... | collective-permute-start | bytes 393224 | tf_op jit(solution)/shard_map/ppermute | solution.py:434
  23.4 4.8 %collective-permute-start.11 = (bf16[6,256,128]{2,1,0:T(8,128)(2,1)S(1)}, bf16[6,256,128]{2,1,0:T(8,128)(2,1)S(1)}, u32[]{:S(2)}, u32[]{:S(2)}) collective-permute-start(bf16[6,256,128]{2,1,0:T(8,128)(2,1)S(1)} %get-tuple-element.78), channel_id=1, source_target_pairs={{0,1},{1,0},{2,3},{3,2},{4,5},{5,4},{6,7},{7,6},{8,9},{9,8},{10,11... | collective-permute-start | bytes 1179656 | tf_op jit(solution)/shard_map/ppermute | solution.py:434
  23.8 7.5 %collective-permute-start.8 = (bf16[384,128]{1,0:T(8,128)(2,1)S(1)}, bf16[384,128]{1,0:T(8,128)(2,1)S(1)}, u32[]{:S(2)}, u32[]{:S(2)}) collective-permute-start(bf16[384,128]{1,0:T(8,128)(2,1)S(1)} %get-tuple-element.73), channel_id=1, source_target_pairs={{0,6},{2,4},{4,2},{6,0},{1,7},{3,5},{5,3},{7,1},{8,14},{10,12},{12... | collective-permute-start | bytes 294920 | tf_op jit(solution)/shard_map/ppermute | solution.py:434
  26.6 8.2 %collective-permute-start.9 = (bf16[384,128]{1,0:T(8,128)(2,1)S(1)}, bf16[384,128]{1,0:T(8,128)(2,1)S(1)}, u32[]{:S(2)}, u32[]{:S(2)}) collective-permute-start(bf16[384,128]{1,0:T(8,128)(2,1)S(1)} %get-tuple-element.74), channel_id=1, source_target_pairs={{0,4},{2,6},{4,0},{6,2},{1,5},{3,7},{5,1},{7,3},{8,12},{10,14},{12... | collective-permute-start | bytes 294920 | tf_op jit(solution)/shard_map/ppermute | solution.py:434
  26.6 8.2 %collective-permute-start.10 = (bf16[384,128]{1,0:T(8,128)(2,1)S(1)}, bf16[384,128]{1,0:T(8,128)(2,1)S(1)}, u32[]{:S(2)}, u32[]{:S(2)}) collective-permute-start(bf16[384,128]{1,0:T(8,128)(2,1)S(1)} %get-tuple-element.75), channel_id=1, source_target_pairs={{0,2},{2,0},{4,6},{6,4},{1,3},{3,1},{5,7},{7,5},{8,10},{10,8},{12,... | collective-permute-start | bytes 294920 | tf_op jit(solution)/shard_map/ppermute | solution.py:434
  28.3 7.7 %copy-start.4 = (s32[256,8]{0,1:T(8,128)S(1)}, s32[256,8]{0,1:T(8,128)}, u32[]{:S(2)}) copy-start(s32[256,8]{0,1:T(8,128)} %param.7) | copy-start | bytes 24580
  28.4 6.5 %collective-permute-start.12 = (bf16[384,128]{1,0:T(8,128)(2,1)S(1)}, bf16[384,128]{1,0:T(8,128)(2,1)S(1)}, u32[]{:S(2)}, u32[]{:S(2)}) collective-permute-start(bf16[384,128]{1,0:T(8,128)(2,1)S(1)} %get-tuple-element.79), channel_id=1, source_target_pairs={{0,24},{8,16},{16,8},{24,0},{1,25},{9,17},{17,9},{25,1},{2,26},{10... | collective-permute-start | bytes 294920 | tf_op jit(solution)/shard_map/ppermute | solution.py:434
  29.9 5.5 %collective-permute-start.13 = (bf16[384,128]{1,0:T(8,128)(2,1)S(1)}, bf16[384,128]{1,0:T(8,128)(2,1)S(1)}, u32[]{:S(2)}, u32[]{:S(2)}) collective-permute-start(bf16[384,128]{1,0:T(8,128)(2,1)S(1)} %get-tuple-element.80), channel_id=1, source_target_pairs={{0,16},{8,24},{16,0},{24,8},{1,17},{9,25},{17,1},{25,9},{2,18},{10... | collective-permute-start | bytes 294920 | tf_op jit(solution)/shard_map/ppermute | solution.py:434
  31.4 4.6 %collective-permute-start.14 = (bf16[384,128]{1,0:T(8,128)(2,1)S(1)}, bf16[384,128]{1,0:T(8,128)(2,1)S(1)}, u32[]{:S(2)}, u32[]{:S(2)}) collective-permute-start(bf16[384,128]{1,0:T(8,128)(2,1)S(1)} %get-tuple-element.81), channel_id=1, source_target_pairs={{0,8},{8,0},{16,24},{24,16},{1,9},{9,1},{17,25},{25,17},{2,10},{10... | collective-permute-start | bytes 294920 | tf_op jit(solution)/shard_map/ppermute | solution.py:434
  36.0 4.1 %copy-start.5 = (bf16[256,32]{0,1:T(8,128)(2,1)S(1)}, bf16[256,32]{0,1:T(8,128)(2,1)}, u32[]{:S(2)}) copy-start(bf16[256,32]{0,1:T(8,128)(2,1)} %param.8) | copy-start | bytes 49156
  36.0 4.1 %copy-start.6 = (bf16[256,32]{0,1:T(8,128)(2,1)S(1)}, bf16[256,32]{0,1:T(8,128)(2,1)}, u32[]{:S(2)}) copy-start(bf16[256,32]{0,1:T(8,128)(2,1)} %param.9) | copy-start | bytes 49156
  36.4 6.9 %collective-permute-start.15 = (bf16[256,128]{1,0:T(8,128)(2,1)S(1)}, bf16[256,128]{1,0:T(8,128)(2,1)S(1)}, u32[]{:S(2)}, u32[]{:S(2)}) collective-permute-start(bf16[256,128]{1,0:T(8,128)(2,1)S(1)} %get-tuple-element.87.refs_2_), channel_id=1, source_target_pairs={{0,4},{2,6},{4,0},{6,2},{1,5},{3,7},{5,1},{7,3},{8,12},{10,14},{12... | collective-permute-start | bytes 196616 | tf_op jit(solution)/shard_map/ppermute | solution.py:434
  37.5 6.6 %collective-permute-start.16 = (bf16[256,128]{1,0:T(8,128)(2,1)S(1)}, bf16[256,128]{1,0:T(8,128)(2,1)S(1)}, u32[]{:S(2)}, u32[]{:S(2)}) collective-permute-start(bf16[256,128]{1,0:T(8,128)(2,1)S(1)} %get-tuple-element.87.refs_2_), channel_id=1, source_target_pairs={{0,6},{2,4},{4,2},{6,0},{1,7},{3,5},{5,3},{7,1},{8,14},{10,12},{12... | collective-permute-start | bytes 196616 | tf_op jit(solution)/shard_map/ppermute | solution.py:434
  40.1 4.6 %collective-permute-start.17 = (bf16[256,128]{1,0:T(8,128)(2,1)S(1)}, bf16[256,128]{1,0:T(8,128)(2,1)S(1)}, u32[]{:S(2)}, u32[]{:S(2)}) collective-permute-start(bf16[256,128]{1,0:T(8,128)(2,1)S(1)} %get-tuple-element.87.refs_2_), channel_id=1, source_target_pairs={{0,2},{2,0},{4,6},{6,4},{1,3},{3,1},{5,7},{7,5},{8,10},{10,8},{12,... | collective-permute-start | bytes 196616 | tf_op jit(solution)/shard_map/ppermute | solution.py:434
  44.8 5.3 %collective-permute-start.18 = (bf16[256,128]{1,0:T(8,128)(2,1)S(1)}, bf16[256,128]{1,0:T(8,128)(2,1)S(1)}, u32[]{:S(2)}, u32[]{:S(2)}) collective-permute-start(bf16[256,128]{1,0:T(8,128)(2,1)S(1)} %sum.1.refs_3_), channel_id=1, source_target_pairs={{0,24},{8,16},{16,8},{24,0},{1,25},{9,17},{17,9},{25,1},{2,26},{10... | collective-permute-start | bytes 196616 | tf_op jit(solution)/shard_map/ppermute | solution.py:434
  46.0 4.8 %collective-permute-start.19 = (bf16[256,128]{1,0:T(8,128)(2,1)S(1)}, bf16[256,128]{1,0:T(8,128)(2,1)S(1)}, u32[]{:S(2)}, u32[]{:S(2)}) collective-permute-start(bf16[256,128]{1,0:T(8,128)(2,1)S(1)} %sum.1.refs_3_), channel_id=1, source_target_pairs={{0,16},{8,24},{16,0},{24,8},{1,17},{9,25},{17,1},{25,9},{2,18},{10... | collective-permute-start | bytes 196616 | tf_op jit(solution)/shard_map/ppermute | solution.py:434
  46.8 4.3 %collective-permute-start.20 = (bf16[256,128]{1,0:T(8,128)(2,1)S(1)}, bf16[256,128]{1,0:T(8,128)(2,1)S(1)}, u32[]{:S(2)}, u32[]{:S(2)}) collective-permute-start(bf16[256,128]{1,0:T(8,128)(2,1)S(1)} %sum.1.refs_3_), channel_id=1, source_target_pairs={{0,8},{8,0},{16,24},{24,16},{1,9},{9,1},{17,25},{25,17},{2,10},{10... | collective-permute-start | bytes 196616 | tf_op jit(solution)/shard_map/ppermute | solution.py:434
  51.1 1.5 %collective-permute-start.21 = (bf16[640,128]{1,0:T(8,128)(2,1)S(1)}, bf16[640,128]{1,0:T(8,128)(2,1)S(1)}, u32[]{:S(2)}, u32[]{:S(2)}) collective-permute-start(bf16[640,128]{1,0:T(8,128)(2,1)S(1)} %join.1.mine_ref), channel_id=1, source_target_pairs={{0,1},{1,0},{2,3},{3,2},{4,5},{5,4},{6,7},{7,6},{8,9},{9,8},{10,11... | collective-permute-start | bytes 491528 | tf_op jit(solution)/shard_map/ppermute | solution.py:434

commit v2 on v1

--- a/solution.py
+++ b/solution.py
@@ -526,10 +526,11 @@
         [((n_row, piece, CZ), BF)],
     )
     rights = spread(rights, "row")
+    order = sorted(range(n_row), key=lambda k: -bin(k).count("1"))
     pay, parts, pieces = call(
         functools.partial(weights_kernel, n_row, n_col),
         "weights",
-        (normed, mask, *lefts[::-1], *rights[::-1]),
+        (normed, mask, *lefts[::-1], *[rights[k] for k in order]),
         (
             shape(4 * PROJ + piece, CZ),
             shape(q, 4 * PROJ, seqs),

time: 53.6 us -> 53.4 us (level)
  waiting for transfers between devices: 15.4 us -> 13.3 us
  starting transfers between devices: 24.3 us -> 26.2 us
    ppermute x22, waiting for transfers between devices: 15.4 us -> 13.3 us  [partner(): return lax.ppermute(value, axis, [(d, d ^ k) for d in range(size)])]
    ppermute x22, starting transfers between devices: 24.3 us -> 26.2 us  [partner(): return lax.ppermute(value, axis, [(d, d ^ k) for d in range(size)])]
  transfers between devices with their start and end apart: 22 -> 22, of which waited for: 15 -> 13; matrix products, arithmetic and copies ran while one was open for 0% -> 0% of each run, Pallas kernels for 12% -> 12%
where the time goes in v2:
time: 53.4 us; the launch traced here: 53.2 us
  starting transfers between devices  26.2 us (49%)
  waiting for transfers between devices  13.3 us (25%)
  Pallas kernels  11.2 us (21%)
  local copies, waits for them, and re-layouts  1.8 us (3%)
  between operations  0.78 us (1%)
    ppermute x22, starting transfers between devices, partner(): return lax.ppermute(value, axis, [(d, d ^ k) for d in range(size)])  26.2 us
    ppermute x22, waiting for transfers between devices, partner(): return lax.ppermute(value, axis, [(d, d ^ k) for d in range(size)])  13.3 us
    pallas_call x15, Pallas kernels, call(): pl.pallas_call(kernel, out_shape=outputs, in_specs=specs(len(inputs), hbm...  11.2 us
    unnamed x14, local copies, waits for them, and re-layouts  1.8 us
  transfers between devices with their start and end apart: 22, of which 13 were waited for; matrix products, arithmetic and copies ran while one was open for 0% of the time, Pallas kernels for 12%

profile of v2, /device:TPU:0, one launch (start us, length us, event | category | flops | bytes accessed | tf_op | source)
XLA Modules:
  0.0 53.2 jit_solution(15371255327296828344)
XLA Ops:
  0.7 2.7 %project.1 = (bf16[272,128]{1,0:T(8,128)(2,1)}, bf16[400,128]{1,0:T(8,128)(2,1)}, bf16[400,128]{1,0:T(8,128)(2,1)}, bf16[400,128]{1,0:T(8,128)(2,1)}, bf16[400,128]{1,0:T(8,128)(2,1)}) custom-call(bf16[1024,256]{1,0:T(8,128)(2,1)} %bitcast.9, s32[8,256]{1,0:T(8,128)} %bitcast.12, bf16[32,256]{1,0:T(8,128)(2,1)} %bitcast.14, bf16[32,256]{1,0:T(8,128)(2,1)} %bitcast.16, ...), custom_call_target="tpu_custom_call" | custom-call | tf_op jit(solution)/shard_map/project/pallas_call | solution.py:383
  3.4 3.0 %collective-permute-start.3 = (bf16[272,128]{1,0:T(8,128)(2,1)}, bf16[272,128]{1,0:T(8,128)(2,1)S(1)}, u32[]{:S(2)}, u32[]{:S(2)}) collective-permute-start(bf16[272,128]{1,0:T(8,128)(2,1)} %get-tuple-element.50.right_ref), channel_id=1, source_target_pairs={{0,8},{8,0},{16,24},{24,16},{1,9},{9,1},{17,25},{25,17},{2,10},{10... | collective-permute-start | bytes 208904 | tf_op jit(solution)/shard_map/ppermute | solution.py:434
  6.4 3.6 %collective-permute-start = (bf16[400,128]{1,0:T(8,128)(2,1)}, bf16[400,128]{1,0:T(8,128)(2,1)S(1)}, u32[]{:S(2)}, u32[]{:S(2)}) collective-permute-start(bf16[400,128]{1,0:T(8,128)(2,1)} %get-tuple-element.54), channel_id=1, source_target_pairs={{0,6},{2,4},{4,2},{6,0},{1,7},{3,5},{5,3},{7,1},{8,14},{10,12},{12... | collective-permute-start | bytes 307208 | tf_op jit(solution)/shard_map/ppermute | solution.py:434
  10.0 0.8 %collective-permute-start.2 = (bf16[400,128]{1,0:T(8,128)(2,1)}, bf16[400,128]{1,0:T(8,128)(2,1)S(1)}, u32[]{:S(2)}, u32[]{:S(2)}) collective-permute-start(bf16[400,128]{1,0:T(8,128)(2,1)} %get-tuple-element.56), channel_id=1, source_target_pairs={{0,2},{2,0},{4,6},{6,4},{1,3},{3,1},{5,7},{7,5},{8,10},{10,8},{12,... | collective-permute-start | bytes 307208 | tf_op jit(solution)/shard_map/ppermute | solution.py:434
  10.7 1.5 %collective-permute-start.4 = (bf16[272,128]{1,0:T(8,128)(2,1)}, bf16[272,128]{1,0:T(8,128)(2,1)S(1)}, u32[]{:S(2)}, u32[]{:S(2)}) collective-permute-start(bf16[272,128]{1,0:T(8,128)(2,1)} %get-tuple-element.50.right_ref), channel_id=1, source_target_pairs={{0,16},{8,24},{16,0},{24,8},{1,17},{9,25},{17,1},{25,9},{2,18},{10... | collective-permute-start | bytes 208904 | tf_op jit(solution)/shard_map/ppermute | solution.py:434
  12.3 0.3 collective-permute-start.5
  12.5 0.9 %copy-done.2 = bf16[400,128]{1,0:T(8,128)(2,1)S(1)} copy-done((bf16[400,128]{1,0:T(8,128)(2,1)S(1)}, bf16[400,128]{1,0:T(8,128)(2,1)}, u32[]{:S(2)}) %copy-start.2) | copy-done | bytes 102424
  13.4 0.9 %copy-done.3 = bf16[272,128]{1,0:T(8,128)(2,1)S(1)} copy-done((bf16[272,128]{1,0:T(8,128)(2,1)S(1)}, bf16[272,128]{1,0:T(8,128)(2,1)}, u32[]{:S(2)}) %copy-start.3) | copy-done | bytes 69656
  14.3 0.3 hold.1
  14.7 0.5 norm.1
  15.2 0.8 %collective-permute-done.4.refs_6_ = bf16[272,128]{1,0:T(8,128)(2,1)S(1)} collective-permute-done((bf16[272,128]{1,0:T(8,128)(2,1)}, bf16[272,128]{1,0:T(8,128)(2,1)S(1)}, u32[]{:S(2)}, u32[]{:S(2)}) %collective-permute-start.4) | collective-permute-done | bytes 69664 | tf_op jit(solution)/shard_map/ppermute | solution.py:434
  16.0 1.7 %collective-permute-done.5.refs_7_ = bf16[272,128]{1,0:T(8,128)(2,1)S(1)} collective-permute-done((bf16[272,128]{1,0:T(8,128)(2,1)}, bf16[272,128]{1,0:T(8,128)(2,1)S(1)}, u32[]{:S(2)}, u32[]{:S(2)}) %collective-permute-start.5) | collective-permute-done | bytes 69664 | tf_op jit(solution)/shard_map/ppermute | solution.py:434
  17.7 0.8 %collective-permute-done.1.refs_1_ = bf16[400,128]{1,0:T(8,128)(2,1)S(1)} collective-permute-done((bf16[400,128]{1,0:T(8,128)(2,1)}, bf16[400,128]{1,0:T(8,128)(2,1)S(1)}, u32[]{:S(2)}, u32[]{:S(2)}) %collective-permute-start.1) | collective-permute-done | bytes 102432 | tf_op jit(solution)/shard_map/ppermute | solution.py:434
  18.5 0.1 pack.1
  18.6 0.1 collective-permute-start.6
  18.7 0.9 %back.1 = (bf16[1024,512]{1,0:T(8,128)(2,1)S(1)}, bf16[128,512]{1,0:T(8,128)(2,1)S(1)}, f32[512,128]{1,0:T(8,128)S(1)}, bf16[1024,128]{1,0:T(8,128)(2,1)S(1)}) custom-call(bf16[1024,128]{1,0:T(8,128)(2,1)S(1)} %get-tuple-element.52.wp, f32[32,256]{1,0:T(8,128)S(1)} %get-tuple-element.59.mr, f32[16,256]{1,0:T(8,128)S(1)} %get-tuple-element.60.ml, ...), custom_call_target="tpu_custom_call" | custom-call | flops 1073741824 | bytes 8388608 | tf_op jit(solution)/shard_map/back/pallas_call | solution.py:383
  19.7 0.8 %collective-permute-done.6.theirs = bf16[6,256,128]{2,1,0:T(8,128)(2,1)S(1)} collective-permute-done((bf16[6,256,128]{2,1,0:T(8,128)(2,1)S(1)}, bf16[6,256,128]{2,1,0:T(8,128)(2,1)S(1)}, u32[]{:S(2)}, u32[]{:S(2)}) %collective-permute-start.6) | collective-permute-done | bytes 393248 | tf_op jit(solution)/shard_map/ppermute | solution.py:434
  20.4 0.7 %left.1 = (bf16[1024,256]{1,0:T(8,128)(2,1)S(1)}, bf16[2,256,128]{2,1,0:T(8,128)(2,1)S(1)}, bf16[2,256,128]{2,1,0:T(8,128)(2,1)S(1)}) custom-call(bf16[1024,128]{1,0:T(8,128)(2,1)S(1)} %get-tuple-element.63.rt_mine, bf16[6,256,128]{2,1,0:T(8,128)(2,1)S(1)} %collective-permute-done.6.theirs, bf16[1024,512]{1,0:T(8,128)(2,1)S(1)} %get-tuple-element.65.dd), custom_call_target="tpu_custom_call" | custom-call | flops 1073741824 | bytes 8388608 | tf_op jit(solution)/shard_map/left/pallas_call | solution.py:383
  21.1 0.2 collective-permute-start.7
  21.3 2.0 %pair.1 = (bf16[6,256,128]{2,1,0:T(8,128)(2,1)S(1)}, bf16[6,256,128]{2,1,0:T(8,128)(2,1)S(1)}, bf16[4,128,128]{2,1,0:T(8,128)(2,1)S(1)}) custom-call(bf16[1024,256]{1,0:T(8,128)(2,1)S(1)} %get-tuple-element.68.rt, bf16[1024,128]{1,0:T(8,128)(2,1)S(1)} %get-tuple-element.52.wp, bf16[1024,512]{1,0:T(8,128)(2,1)S(1)} %get-tuple-element.65.dd, ...), custom_call_target="tpu_custom_call" | custom-call | flops 1073741824 | bytes 8388608 | tf_op jit(solution)/shard_map/pair/pallas_call | solution.py:383
  23.3 0.1 merge_left.1
  23.4 0.4 collective-permute-start.11
  23.8 2.8 %collective-permute-start.8 = (bf16[384,128]{1,0:T(8,128)(2,1)S(1)}, bf16[384,128]{1,0:T(8,128)(2,1)S(1)}, u32[]{:S(2)}, u32[]{:S(2)}) collective-permute-start(bf16[384,128]{1,0:T(8,128)(2,1)S(1)} %get-tuple-element.73), channel_id=1, source_target_pairs={{0,6},{2,4},{4,2},{6,0},{1,7},{3,5},{5,3},{7,1},{8,14},{10,12},{12... | collective-permute-start | bytes 294920 | tf_op jit(solution)/shard_map/ppermute | solution.py:434
  26.6 1.6 %collective-permute-start.10 = (bf16[384,128]{1,0:T(8,128)(2,1)S(1)}, bf16[384,128]{1,0:T(8,128)(2,1)S(1)}, u32[]{:S(2)}, u32[]{:S(2)}) collective-permute-start(bf16[384,128]{1,0:T(8,128)(2,1)S(1)} %get-tuple-element.75), channel_id=1, source_target_pairs={{0,2},{2,0},{4,6},{6,4},{1,3},{3,1},{5,7},{7,5},{8,10},{10,8},{12,... | collective-permute-start | bytes 294920 | tf_op jit(solution)/shard_map/ppermute | solution.py:434
  28.2 0.1 merge_right.1
  28.4 1.6 %collective-permute-start.12 = (bf16[384,128]{1,0:T(8,128)(2,1)S(1)}, bf16[384,128]{1,0:T(8,128)(2,1)S(1)}, u32[]{:S(2)}, u32[]{:S(2)}) collective-permute-start(bf16[384,128]{1,0:T(8,128)(2,1)S(1)} %get-tuple-element.79), channel_id=1, source_target_pairs={{0,24},{8,16},{16,8},{24,0},{1,25},{9,17},{17,9},{25,1},{2,26},{10... | collective-permute-start | bytes 294920 | tf_op jit(solution)/shard_map/ppermute | solution.py:434
  29.9 1.5 %collective-permute-start.13 = (bf16[384,128]{1,0:T(8,128)(2,1)S(1)}, bf16[384,128]{1,0:T(8,128)(2,1)S(1)}, u32[]{:S(2)}, u32[]{:S(2)}) collective-permute-start(bf16[384,128]{1,0:T(8,128)(2,1)S(1)} %get-tuple-element.80), channel_id=1, source_target_pairs={{0,8},{8,0},{16,24},{24,16},{1,9},{9,1},{17,25},{25,17},{2,10},{10... | collective-permute-start | bytes 294920 | tf_op jit(solution)/shard_map/ppermute | solution.py:434
  31.4 1.5 %collective-permute-start.14 = (bf16[384,128]{1,0:T(8,128)(2,1)S(1)}, bf16[384,128]{1,0:T(8,128)(2,1)S(1)}, u32[]{:S(2)}, u32[]{:S(2)}) collective-permute-start(bf16[384,128]{1,0:T(8,128)(2,1)S(1)} %get-tuple-element.81), channel_id=1, source_target_pairs={{0,16},{8,24},{16,0},{24,8},{1,17},{9,25},{17,1},{25,9},{2,18},{10... | collective-permute-start | bytes 294920 | tf_op jit(solution)/shard_map/ppermute | solution.py:434
  32.9 2.0 %collective-permute-done.9.refs_1_ = bf16[384,128]{1,0:T(8,128)(2,1)S(1)} collective-permute-done((bf16[384,128]{1,0:T(8,128)(2,1)S(1)}, bf16[384,128]{1,0:T(8,128)(2,1)S(1)}, u32[]{:S(2)}, u32[]{:S(2)}) %collective-permute-start.9) | collective-permute-done | bytes 98336 | tf_op jit(solution)/shard_map/ppermute | solution.py:434
  34.9 0.6 %collective-permute-done.13.refs_5_ = bf16[384,128]{1,0:T(8,128)(2,1)S(1)} collective-permute-done((bf16[384,128]{1,0:T(8,128)(2,1)S(1)}, bf16[384,128]{1,0:T(8,128)(2,1)S(1)}, u32[]{:S(2)}, u32[]{:S(2)}) %collective-permute-start.13) | collective-permute-done | bytes 98336 | tf_op jit(solution)/shard_map/ppermute | solution.py:434
  35.5 0.5 collective-permute-done.14.refs_6_
  36.0 0.3 weights.1
  36.4 1.3 %collective-permute-start.15 = (bf16[256,128]{1,0:T(8,128)(2,1)S(1)}, bf16[256,128]{1,0:T(8,128)(2,1)S(1)}, u32[]{:S(2)}, u32[]{:S(2)}) collective-permute-start(bf16[256,128]{1,0:T(8,128)(2,1)S(1)} %get-tuple-element.87.refs_2_), channel_id=1, source_target_pairs={{0,4},{2,6},{4,0},{6,2},{1,5},{3,7},{5,1},{7,3},{8,12},{10,14},{12... | collective-permute-start | bytes 196616 | tf_op jit(solution)/shard_map/ppermute | solution.py:434
  37.6 2.5 %collective-permute-start.16 = (bf16[256,128]{1,0:T(8,128)(2,1)S(1)}, bf16[256,128]{1,0:T(8,128)(2,1)S(1)}, u32[]{:S(2)}, u32[]{:S(2)}) collective-permute-start(bf16[256,128]{1,0:T(8,128)(2,1)S(1)} %get-tuple-element.87.refs_2_), channel_id=1, source_target_pairs={{0,6},{2,4},{4,2},{6,0},{1,7},{3,5},{5,3},{7,1},{8,14},{10,12},{12... | collective-permute-start | bytes 196616 | tf_op jit(solution)/shard_map/ppermute | solution.py:434
  40.1 1.7 %input.1 = (bf16[1024,256]{1,0:T(8,128)(2,1)}, f32[8,128]{1,0:T(8,128)S(1)}) custom-call(bf16[1024,256]{1,0:T(8,128)(2,1)S(1)} %bitcast.11, bf16[32,256]{1,0:T(8,128)(2,1)S(1)} %bitcast.15, bf16[32,256]{1,0:T(8,128)(2,1)S(1)} %bitcast.17, bf16[8,128,128]{2,1,0:T(8,128)(2,1)S(1)} %get-tuple-element.85.parts_ref), custom_call_target="tpu_custom_call" | custom-call | flops 268435456 | bytes 2097152 | tf_op jit(solution)/shard_map/input/pallas_call | solution.py:383
  41.8 1.9 %collective-permute-done.15.refs_0_ = bf16[256,128]{1,0:T(8,128)(2,1)S(1)} collective-permute-done((bf16[256,128]{1,0:T(8,128)(2,1)S(1)}, bf16[256,128]{1,0:T(8,128)(2,1)S(1)}, u32[]{:S(2)}, u32[]{:S(2)}) %collective-permute-start.15) | collective-permute-done | bytes 65568 | tf_op jit(solution)/shard_map/ppermute | solution.py:434
  43.7 0.7 %collective-permute-done.17.refs_3_ = bf16[256,128]{1,0:T(8,128)(2,1)S(1)} collective-permute-done((bf16[256,128]{1,0:T(8,128)(2,1)S(1)}, bf16[256,128]{1,0:T(8,128)(2,1)S(1)}, u32[]{:S(2)}, u32[]{:S(2)}) %collective-permute-start.17) | collective-permute-done | bytes 65568 | tf_op jit(solution)/shard_map/ppermute | solution.py:434
  44.4 0.1 sum.1.refs_3_
  44.5 1.5 %collective-permute-start.18 = (bf16[256,128]{1,0:T(8,128)(2,1)S(1)}, bf16[256,128]{1,0:T(8,128)(2,1)S(1)}, u32[]{:S(2)}, u32[]{:S(2)}) collective-permute-start(bf16[256,128]{1,0:T(8,128)(2,1)S(1)} %sum.1.refs_3_), channel_id=1, source_target_pairs={{0,24},{8,16},{16,8},{24,0},{1,25},{9,17},{17,9},{25,1},{2,26},{10... | collective-permute-start | bytes 196616 | tf_op jit(solution)/shard_map/ppermute | solution.py:434
  46.0 0.6 %collective-permute-start.19 = (bf16[256,128]{1,0:T(8,128)(2,1)S(1)}, bf16[256,128]{1,0:T(8,128)(2,1)S(1)}, u32[]{:S(2)}, u32[]{:S(2)}) collective-permute-start(bf16[256,128]{1,0:T(8,128)(2,1)S(1)} %sum.1.refs_3_), channel_id=1, source_target_pairs={{0,16},{8,24},{16,0},{24,8},{1,17},{9,25},{17,1},{25,9},{2,18},{10... | collective-permute-start | bytes 196616 | tf_op jit(solution)/shard_map/ppermute | solution.py:434
  46.6 1.5 %collective-permute-start.20 = (bf16[256,128]{1,0:T(8,128)(2,1)S(1)}, bf16[256,128]{1,0:T(8,128)(2,1)S(1)}, u32[]{:S(2)}, u32[]{:S(2)}) collective-permute-start(bf16[256,128]{1,0:T(8,128)(2,1)S(1)} %sum.1.refs_3_), channel_id=1, source_target_pairs={{0,8},{8,0},{16,24},{24,16},{1,9},{9,1},{17,25},{25,17},{2,10},{10... | collective-permute-start | bytes 196616 | tf_op jit(solution)/shard_map/ppermute | solution.py:434
  48.1 0.7 %place.1 = (bf16[512,128]{1,0:T(8,128)(2,1)}, f32[8,128]{1,0:T(8,128)S(1)}) custom-call(bf16[4,128,128]{2,1,0:T(8,128)(2,1)S(1)} %get-tuple-element.83.couple_ref), custom_call_target="tpu_custom_call" | custom-call | flops 1048576 | bytes 1048576 | tf_op jit(solution)/shard_map/place/pallas_call | solution.py:383
  48.7 1.0 %collective-permute-done.18.refs_0_ = bf16[256,128]{1,0:T(8,128)(2,1)S(1)} collective-permute-done((bf16[256,128]{1,0:T(8,128)(2,1)S(1)}, bf16[256,128]{1,0:T(8,128)(2,1)S(1)}, u32[]{:S(2)}, u32[]{:S(2)}) %collective-permute-start.18) | collective-permute-done | bytes 65568 | tf_op jit(solution)/shard_map/ppermute | solution.py:434
  49.7 0.7 %collective-permute-done.19.refs_1_ = bf16[256,128]{1,0:T(8,128)(2,1)S(1)} collective-permute-done((bf16[256,128]{1,0:T(8,128)(2,1)S(1)}, bf16[256,128]{1,0:T(8,128)(2,1)S(1)}, u32[]{:S(2)}, u32[]{:S(2)}) %collective-permute-start.19) | collective-permute-done | bytes 65568 | tf_op jit(solution)/shard_map/ppermute | solution.py:434
  50.4 0.4 collective-permute-done.20.refs_2_
  50.9 0.1 collective-permute-start.21
  51.0 1.4 %collective-permute-done.21.theirs_ref = bf16[640,128]{1,0:T(8,128)(2,1)S(1)} collective-permute-done((bf16[640,128]{1,0:T(8,128)(2,1)S(1)}, bf16[640,128]{1,0:T(8,128)(2,1)S(1)}, u32[]{:S(2)}, u32[]{:S(2)}) %collective-permute-start.21) | collective-permute-done | bytes 163872 | tf_op jit(solution)/shard_map/ppermute | solution.py:434
  52.4 0.8 %total.1 = (f32[32,256]{1,0:T(8,128)}, f32[32,256]{1,0:T(8,128)}, f32[1024,128]{1,0:T(8,128)}) custom-call(bf16[640,128]{1,0:T(8,128)(2,1)S(1)} %join.1.mine_ref, bf16[640,128]{1,0:T(8,128)(2,1)S(1)} %collective-permute-done.21.theirs_ref), custom_call_target="tpu_custom_call" | custom-call | tf_op jit(solution)/shard_map/total/pallas_call | solution.py:383
  (25 shorter events, 0.1 us)
Async XLA Ops:
  0.6 11.9 %copy-start.1 = (bf16[1024,128]{1,0:T(8,128)(2,1)S(1)}, bf16[1024,128]{1,0:T(8,128)(2,1)}, u32[]{:S(2)}) copy-start(bf16[1024,128]{1,0:T(8,128)(2,1)} %w_ref.1) | copy-start | bytes 786436
  0.6 14.0 %copy-start = (bf16[128,8,256]{2,1,0:T(8,128)(2,1)S(1)}, bf16[128,8,256]{2,1,0:T(8,128)(2,1)}, u32[]{:S(2)}) copy-start(bf16[128,8,256]{2,1,0:T(8,128)(2,1)} %param.6) | copy-start | bytes 1572868
  3.4 8.9 %collective-permute-start.3 = (bf16[272,128]{1,0:T(8,128)(2,1)}, bf16[272,128]{1,0:T(8,128)(2,1)S(1)}, u32[]{:S(2)}, u32[]{:S(2)}) collective-permute-start(bf16[272,128]{1,0:T(8,128)(2,1)} %get-tuple-element.50.right_ref), channel_id=1, source_target_pairs={{0,8},{8,0},{16,24},{24,16},{1,9},{9,1},{17,25},{25,17},{2,10},{10... | collective-permute-start | bytes 208904 | tf_op jit(solution)/shard_map/ppermute | solution.py:434
  6.4 11.3 %collective-permute-start = (bf16[400,128]{1,0:T(8,128)(2,1)}, bf16[400,128]{1,0:T(8,128)(2,1)S(1)}, u32[]{:S(2)}, u32[]{:S(2)}) collective-permute-start(bf16[400,128]{1,0:T(8,128)(2,1)} %get-tuple-element.54), channel_id=1, source_target_pairs={{0,6},{2,4},{4,2},{6,0},{1,7},{3,5},{5,3},{7,1},{8,14},{10,12},{12... | collective-permute-start | bytes 307208 | tf_op jit(solution)/shard_map/ppermute | solution.py:434
  10.0 8.5 %collective-permute-start.1 = (bf16[400,128]{1,0:T(8,128)(2,1)}, bf16[400,128]{1,0:T(8,128)(2,1)S(1)}, u32[]{:S(2)}, u32[]{:S(2)}) collective-permute-start(bf16[400,128]{1,0:T(8,128)(2,1)} %get-tuple-element.55), channel_id=1, source_target_pairs={{0,4},{2,6},{4,0},{6,2},{1,5},{3,7},{5,1},{7,3},{8,12},{10,14},{12... | collective-permute-start | bytes 307208 | tf_op jit(solution)/shard_map/ppermute | solution.py:434
  10.0 8.5 %collective-permute-start.2 = (bf16[400,128]{1,0:T(8,128)(2,1)}, bf16[400,128]{1,0:T(8,128)(2,1)S(1)}, u32[]{:S(2)}, u32[]{:S(2)}) collective-permute-start(bf16[400,128]{1,0:T(8,128)(2,1)} %get-tuple-element.56), channel_id=1, source_target_pairs={{0,2},{2,0},{4,6},{6,4},{1,3},{3,1},{5,7},{7,5},{8,10},{10,8},{12,... | collective-permute-start | bytes 307208 | tf_op jit(solution)/shard_map/ppermute | solution.py:434
  10.7 5.2 %collective-permute-start.4 = (bf16[272,128]{1,0:T(8,128)(2,1)}, bf16[272,128]{1,0:T(8,128)(2,1)S(1)}, u32[]{:S(2)}, u32[]{:S(2)}) collective-permute-start(bf16[272,128]{1,0:T(8,128)(2,1)} %get-tuple-element.50.right_ref), channel_id=1, source_target_pairs={{0,16},{8,24},{16,0},{24,8},{1,17},{9,25},{17,1},{25,9},{2,18},{10... | collective-permute-start | bytes 208904 | tf_op jit(solution)/shard_map/ppermute | solution.py:434
  12.3 5.4 %collective-permute-start.5 = (bf16[272,128]{1,0:T(8,128)(2,1)}, bf16[272,128]{1,0:T(8,128)(2,1)S(1)}, u32[]{:S(2)}, u32[]{:S(2)}) collective-permute-start(bf16[272,128]{1,0:T(8,128)(2,1)} %get-tuple-element.50.right_ref), channel_id=1, source_target_pairs={{0,24},{8,16},{16,8},{24,0},{1,25},{9,17},{17,9},{25,1},{2,26},{10... | collective-permute-start | bytes 208904 | tf_op jit(solution)/shard_map/ppermute | solution.py:434
  12.5 0.9 %copy-start.2 = (bf16[400,128]{1,0:T(8,128)(2,1)S(1)}, bf16[400,128]{1,0:T(8,128)(2,1)}, u32[]{:S(2)}) copy-start(bf16[400,128]{1,0:T(8,128)(2,1)} %get-tuple-element.51.left_ref) | copy-start | bytes 307204
  13.4 0.9 %copy-start.3 = (bf16[272,128]{1,0:T(8,128)(2,1)S(1)}, bf16[272,128]{1,0:T(8,128)(2,1)}, u32[]{:S(2)}) copy-start(bf16[272,128]{1,0:T(8,128)(2,1)} %get-tuple-element.50.right_ref) | copy-start | bytes 208900
  18.6 1.8 %collective-permute-start.6 = (bf16[6,256,128]{2,1,0:T(8,128)(2,1)S(1)}, bf16[6,256,128]{2,1,0:T(8,128)(2,1)S(1)}, u32[]{:S(2)}, u32[]{:S(2)}) collective-permute-start(bf16[6,256,128]{2,1,0:T(8,128)(2,1)S(1)} %get-tuple-element.64), channel_id=1, source_target_pairs={{0,1},{1,0},{2,3},{3,2},{4,5},{5,4},{6,7},{7,6},{8,9},{9,8},{10,11... | collective-permute-start | bytes 1179656 | tf_op jit(solution)/shard_map/ppermute | solution.py:434
  21.1 2.2 %collective-permute-start.7 = (bf16[2,256,128]{2,1,0:T(8,128)(2,1)S(1)}, bf16[2,256,128]{2,1,0:T(8,128)(2,1)S(1)}, u32[]{:S(2)}, u32[]{:S(2)}) collective-permute-start(bf16[2,256,128]{2,1,0:T(8,128)(2,1)S(1)} %get-tuple-element.67), channel_id=1, source_target_pairs={{0,1},{1,0},{2,3},{3,2},{4,5},{5,4},{6,7},{7,6},{8,9},{9,8},{10,11... | collective-permute-start | bytes 393224 | tf_op jit(solution)/shard_map/ppermute | solution.py:434
  23.4 4.8 %collective-permute-start.11 = (bf16[6,256,128]{2,1,0:T(8,128)(2,1)S(1)}, bf16[6,256,128]{2,1,0:T(8,128)(2,1)S(1)}, u32[]{:S(2)}, u32[]{:S(2)}) collective-permute-start(bf16[6,256,128]{2,1,0:T(8,128)(2,1)S(1)} %get-tuple-element.78), channel_id=1, source_target_pairs={{0,1},{1,0},{2,3},{3,2},{4,5},{5,4},{6,7},{7,6},{8,9},{9,8},{10,11... | collective-permute-start | bytes 1179656 | tf_op jit(solution)/shard_map/ppermute | solution.py:434
  23.8 7.6 %collective-permute-start.8 = (bf16[384,128]{1,0:T(8,128)(2,1)S(1)}, bf16[384,128]{1,0:T(8,128)(2,1)S(1)}, u32[]{:S(2)}, u32[]{:S(2)}) collective-permute-start(bf16[384,128]{1,0:T(8,128)(2,1)S(1)} %get-tuple-element.73), channel_id=1, source_target_pairs={{0,6},{2,4},{4,2},{6,0},{1,7},{3,5},{5,3},{7,1},{8,14},{10,12},{12... | collective-permute-start | bytes 294920 | tf_op jit(solution)/shard_map/ppermute | solution.py:434
  26.6 8.2 %collective-permute-start.9 = (bf16[384,128]{1,0:T(8,128)(2,1)S(1)}, bf16[384,128]{1,0:T(8,128)(2,1)S(1)}, u32[]{:S(2)}, u32[]{:S(2)}) collective-permute-start(bf16[384,128]{1,0:T(8,128)(2,1)S(1)} %get-tuple-element.74), channel_id=1, source_target_pairs={{0,4},{2,6},{4,0},{6,2},{1,5},{3,7},{5,1},{7,3},{8,12},{10,14},{12... | collective-permute-start | bytes 294920 | tf_op jit(solution)/shard_map/ppermute | solution.py:434
  26.6 8.2 %collective-permute-start.10 = (bf16[384,128]{1,0:T(8,128)(2,1)S(1)}, bf16[384,128]{1,0:T(8,128)(2,1)S(1)}, u32[]{:S(2)}, u32[]{:S(2)}) collective-permute-start(bf16[384,128]{1,0:T(8,128)(2,1)S(1)} %get-tuple-element.75), channel_id=1, source_target_pairs={{0,2},{2,0},{4,6},{6,4},{1,3},{3,1},{5,7},{7,5},{8,10},{10,8},{12,... | collective-permute-start | bytes 294920 | tf_op jit(solution)/shard_map/ppermute | solution.py:434
  28.3 7.7 %copy-start.4 = (s32[256,8]{0,1:T(8,128)S(1)}, s32[256,8]{0,1:T(8,128)}, u32[]{:S(2)}) copy-start(s32[256,8]{0,1:T(8,128)} %param.7) | copy-start | bytes 24580
  28.4 6.5 %collective-permute-start.12 = (bf16[384,128]{1,0:T(8,128)(2,1)S(1)}, bf16[384,128]{1,0:T(8,128)(2,1)S(1)}, u32[]{:S(2)}, u32[]{:S(2)}) collective-permute-start(bf16[384,128]{1,0:T(8,128)(2,1)S(1)} %get-tuple-element.79), channel_id=1, source_target_pairs={{0,24},{8,16},{16,8},{24,0},{1,25},{9,17},{17,9},{25,1},{2,26},{10... | collective-permute-start | bytes 294920 | tf_op jit(solution)/shard_map/ppermute | solution.py:434
  29.9 5.6 %collective-permute-start.13 = (bf16[384,128]{1,0:T(8,128)(2,1)S(1)}, bf16[384,128]{1,0:T(8,128)(2,1)S(1)}, u32[]{:S(2)}, u32[]{:S(2)}) collective-permute-start(bf16[384,128]{1,0:T(8,128)(2,1)S(1)} %get-tuple-element.80), channel_id=1, source_target_pairs={{0,8},{8,0},{16,24},{24,16},{1,9},{9,1},{17,25},{25,17},{2,10},{10... | collective-permute-start | bytes 294920 | tf_op jit(solution)/shard_map/ppermute | solution.py:434
  31.4 4.6 %collective-permute-start.14 = (bf16[384,128]{1,0:T(8,128)(2,1)S(1)}, bf16[384,128]{1,0:T(8,128)(2,1)S(1)}, u32[]{:S(2)}, u32[]{:S(2)}) collective-permute-start(bf16[384,128]{1,0:T(8,128)(2,1)S(1)} %get-tuple-element.81), channel_id=1, source_target_pairs={{0,16},{8,24},{16,0},{24,8},{1,17},{9,25},{17,1},{25,9},{2,18},{10... | collective-permute-start | bytes 294920 | tf_op jit(solution)/shard_map/ppermute | solution.py:434
  36.0 4.1 %copy-start.5 = (bf16[256,32]{0,1:T(8,128)(2,1)S(1)}, bf16[256,32]{0,1:T(8,128)(2,1)}, u32[]{:S(2)}) copy-start(bf16[256,32]{0,1:T(8,128)(2,1)} %param.8) | copy-start | bytes 49156
  36.0 4.1 %copy-start.6 = (bf16[256,32]{0,1:T(8,128)(2,1)S(1)}, bf16[256,32]{0,1:T(8,128)(2,1)}, u32[]{:S(2)}) copy-start(bf16[256,32]{0,1:T(8,128)(2,1)} %param.9) | copy-start | bytes 49156
  36.4 7.3 %collective-permute-start.15 = (bf16[256,128]{1,0:T(8,128)(2,1)S(1)}, bf16[256,128]{1,0:T(8,128)(2,1)S(1)}, u32[]{:S(2)}, u32[]{:S(2)}) collective-permute-start(bf16[256,128]{1,0:T(8,128)(2,1)S(1)} %get-tuple-element.87.refs_2_), channel_id=1, source_target_pairs={{0,4},{2,6},{4,0},{6,2},{1,5},{3,7},{5,1},{7,3},{8,12},{10,14},{12... | collective-permute-start | bytes 196616 | tf_op jit(solution)/shard_map/ppermute | solution.py:434
  37.6 6.1 %collective-permute-start.16 = (bf16[256,128]{1,0:T(8,128)(2,1)S(1)}, bf16[256,128]{1,0:T(8,128)(2,1)S(1)}, u32[]{:S(2)}, u32[]{:S(2)}) collective-permute-start(bf16[256,128]{1,0:T(8,128)(2,1)S(1)} %get-tuple-element.87.refs_2_), channel_id=1, source_target_pairs={{0,6},{2,4},{4,2},{6,0},{1,7},{3,5},{5,3},{7,1},{8,14},{10,12},{12... | collective-permute-start | bytes 196616 | tf_op jit(solution)/shard_map/ppermute | solution.py:434
  40.1 4.3 %collective-permute-start.17 = (bf16[256,128]{1,0:T(8,128)(2,1)S(1)}, bf16[256,128]{1,0:T(8,128)(2,1)S(1)}, u32[]{:S(2)}, u32[]{:S(2)}) collective-permute-start(bf16[256,128]{1,0:T(8,128)(2,1)S(1)} %get-tuple-element.87.refs_2_), channel_id=1, source_target_pairs={{0,2},{2,0},{4,6},{6,4},{1,3},{3,1},{5,7},{7,5},{8,10},{10,8},{12,... | collective-permute-start | bytes 196616 | tf_op jit(solution)/shard_map/ppermute | solution.py:434
  44.5 5.2 %collective-permute-start.18 = (bf16[256,128]{1,0:T(8,128)(2,1)S(1)}, bf16[256,128]{1,0:T(8,128)(2,1)S(1)}, u32[]{:S(2)}, u32[]{:S(2)}) collective-permute-start(bf16[256,128]{1,0:T(8,128)(2,1)S(1)} %sum.1.refs_3_), channel_id=1, source_target_pairs={{0,24},{8,16},{16,8},{24,0},{1,25},{9,17},{17,9},{25,1},{2,26},{10... | collective-permute-start | bytes 196616 | tf_op jit(solution)/shard_map/ppermute | solution.py:434
  46.0 4.4 %collective-permute-start.19 = (bf16[256,128]{1,0:T(8,128)(2,1)S(1)}, bf16[256,128]{1,0:T(8,128)(2,1)S(1)}, u32[]{:S(2)}, u32[]{:S(2)}) collective-permute-start(bf16[256,128]{1,0:T(8,128)(2,1)S(1)} %sum.1.refs_3_), channel_id=1, source_target_pairs={{0,16},{8,24},{16,0},{24,8},{1,17},{9,25},{17,1},{25,9},{2,18},{10... | collective-permute-start | bytes 196616 | tf_op jit(solution)/shard_map/ppermute | solution.py:434
  46.6 4.3 %collective-permute-start.20 = (bf16[256,128]{1,0:T(8,128)(2,1)S(1)}, bf16[256,128]{1,0:T(8,128)(2,1)S(1)}, u32[]{:S(2)}, u32[]{:S(2)}) collective-permute-start(bf16[256,128]{1,0:T(8,128)(2,1)S(1)} %sum.1.refs_3_), channel_id=1, source_target_pairs={{0,8},{8,0},{16,24},{24,16},{1,9},{9,1},{17,25},{25,17},{2,10},{10... | collective-permute-start | bytes 196616 | tf_op jit(solution)/shard_map/ppermute | solution.py:434
  50.9 1.5 %collective-permute-start.21 = (bf16[640,128]{1,0:T(8,128)(2,1)S(1)}, bf16[640,128]{1,0:T(8,128)(2,1)S(1)}, u32[]{:S(2)}, u32[]{:S(2)}) collective-permute-start(bf16[640,128]{1,0:T(8,128)(2,1)S(1)} %join.1.mine_ref), channel_id=1, source_target_pairs={{0,1},{1,0},{2,3},{3,2},{4,5},{5,4},{6,7},{7,6},{8,9},{9,8},{10,11... | collective-permute-start | bytes 491528 | tf_op jit(solution)/shard_map/ppermute | solution.py:434
